TPU v7x, 256 devices: a whole 4x4x8 slice. The times are simulated.
256 devices in a mesh: seq: 64 (over y, z, core), dp: 4 (over x).
Axes of the slice: x: 4, y: 4, z: 8, core: 2. Of those that a mesh axis runs over, the one named last changes fastest.
Arguments:
- streams: bfloat16 [4, 8192, 3, 4096], P('dp', 'seq'), may hold values from -6 to 6
- cotangent: bfloat16 [4, 8192, 4096], P('dp', 'seq'), may hold values from -6 to 6
- doc_ids: int32 [4, 8192], P('dp', 'seq'), may hold values from 0 to 63, never falling along the last dimension, each value on 1 to 512 neighbouring positions
- short_taps: float32 [3, 3, 4096], P(None, None, 'seq'), may hold values from -3.5 to 3.5
- long_taps: float32 [256, 128], P('seq'), may hold values from -0.5 to 0.5
- skip_gain: float32 [4096], P('seq'), may hold values from 0.5 to 1.5
Outputs:
- mixed_out: bfloat16 [4, 8192, 4096], P('dp', 'seq')
- stream_grad: bfloat16 [4, 8192, 3, 4096], P('dp', 'seq')
- short_grad: float32 [3, 3, 4096], P(None, None, 'seq')
- taps_grad: float32 [256, 128], P('seq')
- gain_grad: float32 [4096], P('seq')
Inputs may be any that keep to these rules, and one draw needn't show every extreme that they name: `doc_ids`: along each packed sequence the ids start at 0, never fall and rise by one at each document start; each document has 1 to 512 tokens, and one has exactly 512.
All inputs are finite; a program needn't handle non-finite values.
Results may differ from a plain program's by a relative error of at most 0.005.
Values may be sent and summed in bfloat16 or wider, within the bound.
A program may use at most 256 MiB of HBM per device.

v0:
```python
import math

import jax
import jax.numpy as jnp
from jax import lax
from jax.sharding import PartitionSpec as P


def banded(pattern, row_count):
    groups, extent = pattern.shape
    padded = jnp.concatenate([pattern, jnp.zeros((groups, 1), pattern.dtype)], axis=1)
    flattened = jnp.tile(padded, (1, row_count))[:, : row_count * extent]
    return flattened.reshape(groups, row_count, extent)


def windowed(extended, tap_count):
    earlier = extended[:-tap_count].reshape((-1, tap_count) + extended.shape[1:])
    later_rows = extended[tap_count:].reshape((-1, tap_count) + extended.shape[1:])
    return jnp.concatenate([earlier, later_rows], axis=1)


def turn_layout(blocks, groups, turn_limit):
    per_turn = min(4, blocks)
    span_groups = math.gcd(groups, max(1, turn_limit // per_turn))
    return (per_turn, span_groups)


def to_turns(inputs, per_turn, span_groups):
    blocks, row_count, groups, group_width = inputs.shape
    group_spans = groups // span_groups
    reshaped = inputs.reshape(
        blocks // per_turn, per_turn, row_count, group_spans, span_groups, group_width
    )
    reshaped = jnp.transpose(reshaped, (3, 0, 1, 2, 4, 5))
    return reshaped.reshape(
        group_spans * (blocks // per_turn), per_turn, row_count, span_groups, group_width
    )


def from_turns(result, blocks, groups):
    turn_total, per_turn, row_count, span_groups, group_width = result.shape
    group_spans = groups // span_groups
    merged = result.reshape(
        group_spans, blocks // per_turn, per_turn, row_count, span_groups, group_width
    )
    merged = jnp.transpose(merged, (1, 2, 3, 0, 4, 5))
    return merged.reshape(blocks * row_count, groups * group_width)


def ids_to_turns(id_windows, per_turn, group_spans):
    reshaped = id_windows.reshape(-1, per_turn, id_windows.shape[1])
    return jnp.tile(reshaped, (group_spans, 1, 1))


def conv_blocks(extended, id_ext, kernel, own_start, turn_limit):
    groups, tap_count = (kernel.shape[0], kernel.shape[1])
    length = extended.shape[0] - tap_count
    channels = extended.shape[1]
    blocks = length // tap_count
    per_turn, span_groups = turn_layout(blocks, groups, turn_limit)
    block_turns = blocks // per_turn
    group_spans = groups // span_groups
    inputs = windowed(extended, tap_count).reshape(
        blocks, 2 * tap_count, groups, channels // groups
    )
    data_turns = to_turns(inputs, per_turn, span_groups)
    id_turns = ids_to_turns(windowed(id_ext, tap_count), per_turn, group_spans)
    kernel_spans = kernel.reshape(group_spans, span_groups, kernel.shape[1], kernel.shape[2])
    span_index = jnp.arange(group_spans * block_turns, dtype=jnp.int32) // block_turns

    def conv_one_turn(operands):
        data_win, ids_win, which = operands
        kernel_part = lax.dynamic_index_in_dim(kernel_spans, which, 0, keepdims=False)
        own_ids = ids_win[:, own_start : own_start + tap_count]
        same_doc = (own_ids[:, :, None] == ids_win[:, None, :]).astype(kernel_part.dtype)
        masked = kernel_part[None] * same_doc[:, None]
        return jnp.einsum("ngts,nsgc->ntgc", masked, data_win, preferred_element_type=jnp.float32)

    result = lax.map(conv_one_turn, (data_turns, id_turns, span_index))
    return from_turns(result, blocks, groups)


def long_forward(gated_ext, id_ext, taps16, turn_limit):
    groups, tap_count = taps16.shape
    pattern = jnp.concatenate(
        [
            jnp.zeros((groups, 1), taps16.dtype),
            taps16[:, ::-1],
            jnp.zeros((groups, tap_count - 1), taps16.dtype),
        ],
        axis=1,
    )
    return conv_blocks(gated_ext, id_ext, banded(pattern, tap_count), tap_count, turn_limit)


def long_backward(grad_ext, id_ext, taps16, turn_limit):
    groups, tap_count = taps16.shape
    pattern = jnp.concatenate([taps16, jnp.zeros((groups, tap_count), taps16.dtype)], axis=1)
    return conv_blocks(grad_ext, id_ext, banded(pattern, tap_count), 0, turn_limit)


def long_taps_grad(grad16, gated_ext, id_ext, groups, turn_limit):
    length, channels = grad16.shape
    tap_count = gated_ext.shape[0] - length
    blocks = length // tap_count
    group_width = channels // groups
    per_turn, span_groups = turn_layout(blocks, groups, turn_limit)
    group_spans = groups // span_groups
    grad_turns = to_turns(
        grad16.reshape(blocks, tap_count, groups, group_width), per_turn, span_groups
    )
    data_turns = to_turns(
        windowed(gated_ext, tap_count).reshape(blocks, 2 * tap_count, groups, group_width),
        per_turn,
        span_groups,
    )
    id_turns = ids_to_turns(windowed(id_ext, tap_count), per_turn, group_spans)

    def long_one_turn(operands):
        grad_part, data_win, ids_win = operands
        product = jnp.einsum(
            "ntgc,nsgc->ngts", grad_part, data_win, preferred_element_type=jnp.float32
        )
        same_doc = (ids_win[:, tap_count:, None] == ids_win[:, None, :]).astype(jnp.float32)
        return jnp.sum(product * same_doc[:, None], axis=0)

    partial_sums = lax.map(long_one_turn, (grad_turns, data_turns, id_turns))
    summed = jnp.sum(
        partial_sums.reshape(group_spans, -1, span_groups, tap_count, 2 * tap_count), axis=1
    )
    flattened = summed.reshape(groups, tap_count * 2 * tap_count)
    flattened = jnp.concatenate([flattened, jnp.zeros((groups, tap_count), jnp.float32)], axis=1)
    skewed = flattened.reshape(groups, tap_count, 2 * tap_count + 1)
    return jnp.sum(skewed[:, :, 1 : tap_count + 1], axis=1)[:, ::-1]


def short_forward(stream_ext, id_ext, short_taps):
    short_lead = short_taps.shape[1] - 1
    length = stream_ext.shape[0] - short_lead
    own_ids = id_ext[short_lead:]
    summed = jnp.zeros((length,) + stream_ext.shape[1:], jnp.float32)
    for offset in range(short_lead + 1):
        start_row = short_lead - offset
        same_doc = (id_ext[start_row : start_row + length] == own_ids).astype(jnp.float32)
        summed = (
            summed
            + short_taps[:, offset][None]
            * stream_ext[start_row : start_row + length]
            * same_doc[:, None, None]
        )
    return summed


def short_backward(grad_ext, id_ext, short_taps):
    short_lead = short_taps.shape[1] - 1
    length = grad_ext.shape[0] - short_lead
    own_ids = id_ext[:length]
    summed = jnp.zeros((length,) + grad_ext.shape[1:], jnp.float32)
    for offset in range(short_lead + 1):
        same_doc = (id_ext[offset : offset + length] == own_ids).astype(jnp.float32)
        summed = (
            summed
            + short_taps[:, offset][None]
            * grad_ext[offset : offset + length]
            * same_doc[:, None, None]
        )
    return summed


def short_taps_grad(act_grad, stream_ext, id_ext, short_count):
    short_lead = short_count - 1
    length = act_grad.shape[0]
    own_ids = id_ext[short_lead:]
    pieces = []
    for offset in range(short_count):
        start_row = short_lead - offset
        same_doc = (id_ext[start_row : start_row + length] == own_ids).astype(jnp.float32)
        pieces.append(
            jnp.sum(
                act_grad * stream_ext[start_row : start_row + length] * same_doc[:, None, None],
                axis=0,
            )
        )
    return jnp.stack(pieces, axis=1)


def filler_ids(amount):
    return jnp.full((amount,), -1, jnp.int32)


def one_sequence(streams, cotangent, doc_ids, short_taps, long_taps, skip_gain):
    length, channels = cotangent.shape
    groups, tap_count = long_taps.shape
    short_lead = short_taps.shape[1] - 1
    turn_limit = 16
    stream_ext = jnp.concatenate(
        [jnp.zeros((short_lead,) + streams.shape[1:], jnp.float32), streams.astype(jnp.float32)],
        axis=0,
    )
    short_ids = jnp.concatenate([filler_ids(short_lead), doc_ids])
    activated = short_forward(stream_ext, short_ids, short_taps)
    query_act, key_act, value_act = (activated[:, 0], activated[:, 1], activated[:, 2])
    gated_input = key_act * value_act
    gated16 = gated_input.astype(jnp.bfloat16)
    taps16 = long_taps.astype(jnp.bfloat16)
    gated_ext = jnp.concatenate([jnp.zeros((tap_count, channels), jnp.bfloat16), gated16], axis=0)
    long_ids = jnp.concatenate([filler_ids(tap_count), doc_ids])
    convolved = long_forward(gated_ext, long_ids, taps16, turn_limit) + skip_gain * gated_input
    mixed_out = (query_act * convolved).astype(jnp.bfloat16)
    cot_float = cotangent.astype(jnp.float32)
    conv_grad = cot_float * query_act
    conv_grad16 = conv_grad.astype(jnp.bfloat16)
    grad_ext = jnp.concatenate(
        [conv_grad16, jnp.zeros((tap_count, channels), jnp.bfloat16)], axis=0
    )
    after_ids = jnp.concatenate([doc_ids, filler_ids(tap_count)])
    gated_grad = long_backward(grad_ext, after_ids, taps16, turn_limit) + skip_gain * conv_grad
    taps_grad = long_taps_grad(conv_grad16, gated_ext, long_ids, groups, turn_limit)
    gain_grad = jnp.sum(conv_grad * gated_input, axis=0)
    act_grad = jnp.stack(
        [cot_float * convolved, gated_grad * value_act, gated_grad * key_act], axis=1
    )
    act_ext = jnp.concatenate([act_grad, jnp.zeros((short_lead, 3, channels), jnp.float32)], axis=0)
    stream_grad = short_backward(act_ext, after_ids[: length + short_lead], short_taps).astype(
        jnp.bfloat16
    )
    short_grad = short_taps_grad(act_grad, stream_ext, short_ids, short_lead + 1)
    return (mixed_out, stream_grad, short_grad, taps_grad, gain_grad)


def local(streams, cotangent, doc_ids, short_taps, long_taps, skip_gain):
    local_rows = streams.shape[1]
    all_ids = lax.all_gather(doc_ids, "seq", axis=1, tiled=True)[0]
    channel_streams, channel_cot = (
        lax.all_to_all(streams, "seq", split_axis=3, concat_axis=1, tiled=True),
        lax.all_to_all(cotangent[:, :, None, :], "seq", split_axis=3, concat_axis=1, tiled=True),
    )
    local_out, local_grad, short_grad, taps_grad, gain_grad = one_sequence(
        channel_streams[0], channel_cot[0, :, 0, :], all_ids, short_taps, long_taps, skip_gain
    )
    back_out, back_grad = (
        lax.all_to_all(local_out[None, :, None, :], "seq", split_axis=1, concat_axis=3, tiled=True),
        lax.all_to_all(local_grad[None], "seq", split_axis=1, concat_axis=3, tiled=True),
    )
    mixed_out = back_out[:, :, 0, :]
    short_grad, taps_grad, gain_grad = lax.psum((short_grad, taps_grad, gain_grad), "dp")
    grad_scale = 1.0 / math.sqrt(lax.axis_size("dp") * lax.axis_size("seq") * local_rows)
    return (
        mixed_out,
        back_grad,
        short_grad * grad_scale,
        taps_grad * grad_scale,
        gain_grad * grad_scale,
    )


def solution(mesh):
    return jax.shard_map(
        local,
        mesh=mesh,
        in_specs=(
            P("dp", "seq", None, None),
            P("dp", "seq", None),
            P("dp", "seq"),
            P(None, None, "seq"),
            P("seq", None),
            P("seq"),
        ),
        out_specs=(
            P("dp", "seq", None),
            P("dp", "seq", None, None),
            P(None, None, "seq"),
            P("seq", None),
            P("seq"),
        ),
        check_vma=False,
    )
```

profile of v0, /device:TPU:1, one launch (start us, length us, event | category | flops | bytes accessed | tf_op | source)
XLA Modules:
  0.0 618.8 jit_solution(15938540570190511147)
XLA Ops:
  0.6 5.0 copy.72
  6.2 22.4 %reduce.3 = bf16[4096,128]{1,0:T(8,128)(2,1)S(1)} reduce(bf16[4096,1,1,128]{3,2,1,0:T(2,128)(2,1)S(1)} %bitcast.198, bf16[]{:T(256)} %broadcast.124), dimensions={1,2}, to_apply=%bitcast.154.reduce_sub_computation | reduce | bytes 2097154
  29.7 13.2 %all-to-all-start.2 = ((bf16[64,2,4096]{2,1,0:T(2,128)(2,1)}), bf16[64,2,4096]{2,1,0:T(2,128)(2,1)S(1)}, u32[]{:S(2)}, u32[]{:S(2)}) async-start(bf16[64,2,4096]{2,1,0:T(2,128)(2,1)} %reshape.219), calls=%async_computation.2 | async-start | bytes 2097152 | tf_op jit(solution)/shard_map/all_to_all | solution.py:236
  42.9 7.2 %copy.64 = bf16[1,128,3,4096]{1,2,0,3:T(4,128)(2,1)} copy(bf16[1,128,3,4096]{3,1,2,0:T(8,128)(2,1)} %param.12) | data formatting | bytes 6291456 | tf_op args[0]
  50.0 21.4 %all-to-all-done.2 = bf16[64,2,4096]{2,1,0:T(2,128)(2,1)S(1)} async-done(((bf16[64,2,4096]{2,1,0:T(2,128)(2,1)}), bf16[64,2,4096]{2,1,0:T(2,128)(2,1)S(1)}, u32[]{:S(2)}, u32[]{:S(2)}) %all-to-all-start.2) | async-done | bytes 1048608 | tf_op jit(solution)/shard_map/all_to_all | solution.py:236
  71.4 6.4 %all-to-all-start = ((bf16[1,128,3,4096]{1,2,0,3:T(4,128)(2,1)}), bf16[1,128,3,4096]{1,2,0,3:T(4,128)(2,1)}, u32[]{:S(2)}, u32[]{:S(2)}) async-start(bf16[1,128,3,4096]{1,2,0,3:T(4,128)(2,1)} %copy.64), calls=%async_computation | async-start | bytes 8388608 | tf_op jit(solution)/shard_map/all_to_all | solution.py:235
  80.7 123.0 %all_gather.3 = s32[1,8192]{1,0:T(1,128)S(1)} all-gather(s32[1,128]{1,0:T(1,128)S(1)} %copy-done.14), channel_id=1, replica_groups=mesh['seq'=64,'dp'=4] {'seq'}, dimensions={1}, use_global_device_ids=true | all-gather | bytes 33280 | tf_op jit(solution)/shard_map/all_gather | solution.py:233
  213.3 4.7 convert_bitcast_fusion
  218.0 6.2 %copy.66 = f32[1,64,128,3,64]{2,1,4,3,0:T(8,128)} copy(f32[1,64,128,3,64]{2,4,1,3,0:T(8,128)S(1)} %get-tuple-element.216) | data formatting | bytes 12582912 | tf_op jit(solution)/shard_map/convert_element_type | solution.py:197
  224.2 7.2 %reshape.208 = f32[8192,3,64]{0,2,1:T(8,128)} reshape(f32[1,64,128,3,64]{2,1,4,3,0:T(8,128)} %copy.66) | data formatting | bytes 12582912 | tf_op jit(solution)/shard_map/convert_element_type | solution.py:197
  231.4 8.6 %multiply_add_fusion = f32[8192,3,64]{0,2,1:T(8,128)S(1)} fusion(f32[8192,3,64]{0,2,1:T(8,128)} %reshape.208, f32[8192]{0:T(1024)S(1)} %get-tuple-element.228, f32[3,64]{1,0:T(4,128)S(1)} %get-tuple-element.236, f32[8192]{0:T(1024)S(1)} %get-tuple-element.229, f32[3,64]{1,0:T(4,128)S(1)} %get-tuple-element.237, f32[3,64]{1,0:T(4,128)S(1)} %bitcast.219), kind=kLoop, calls=%fused_computation.35 | loop fusion | flops 11010048 | bytes 12650752 | tf_op jit(solution)/shard_map/add | solution.py:146
  260.0 37.3 %while.32 = (s32[]{:T(128)}, f32[16,4,128,4,16]{2,1,0,4,3:T(4,128)}, bf16[16,4,256,4,16]{2,4,3,1,0:T(8,128)(2,1)}, bf16[1,4,128,256]{3,2,1,0:T(8,128)(2,1)}, s32[16,4,256]{2,1,0:T(4,128)S(1)}, /*index=5*/s32[]{:T(128)}) while((s32[]{:T(128)}, f32[16,4,128,4,16]{2,1,0,4,3:T(4,128)}, bf16[16,4,256,4,16]{2,4,3,1,0:T(8,128)(2,1)}, ...), condition=%wide.region_1.2_spmd, body=%wide.region_0.1_spmd.sunk | while | flops 17563648 | bytes 1329241 | solution.py:79
  307.2 3.8 squeeze.54
  311.1 3.9 fusion.18
  319.8 47.0 %while.33 = (s32[]{:T(128)}, f32[16,4,128,4,16]{2,1,0,4,3:T(4,128)}, bf16[16,4,256,4,16]{2,1,0,4,3:T(4,128)(2,1)}, bf16[1,4,128,256]{3,2,1,0:T(8,128)(2,1)S(1)}, s32[16,4,256]{2,1,0:T(4,128)}, /*index=5*/s32[]{:T(128)}) while((s32[]{:T(128)}, f32[16,4,128,4,16]{2,1,0,4,3:T(4,128)}, bf16[16,4,256,4,16]{2,1,0,4,3:T(4,128)(2,1)}, ...), condition=%wide.region_3.4_spmd, body=%wide.region_2.3_spmd.sunk | while | flops 17563648 | bytes 1591385 | solution.py:79
  374.4 6.6 %slice_multiply_fusion = (f32[8192,1,64]{0,2,1:T(8,128)}, f32[8192,1,64]{0,2,1:T(8,128)S(1)}, f32[8192,1,64]{0,2,1:T(8,128)}) fusion(f32[8192,3,64]{0,2,1:T(8,128)} %copy-done, f32[8192,1,64]{0,2,1:T(8,128)S(1)} %copy-done.7, f32[8192,1,64]{0,1,2:T(1,128)S(1)} %bitcast.203, f32[64]{0:T(128)S(1)} %copy-done.13, f32[8192,1,64]{0,2,1:T(8,128)S(1)} %copy-done.6, ...), kind=kLoop, calls=%fused_computation.53 | loop fusion | flops 3670016 | bytes 18874624 | tf_op jit(solution)/shard_map/mul | solution.py:221
  382.9 9.2 %copy.69 = bf16[1,8192,1,64]{3,2,0,1:T(2,128)(2,1)} copy(bf16[1,8192,1,64]{1,3,2,0:T(8,128)(2,1)} %fusion.16) | data formatting | bytes 2097152 | tf_op jit(solution)/shard_map/convert_element_type | solution.py:209
  392.1 46.7 %reduce.4 = bf16[8192,64]{1,0:T(8,128)(2,1)} reduce(bf16[8192,1,1,64]{3,2,1,0:T(2,128)(2,1)} %bitcast.190, bf16[]{:T(256)} %broadcast.124), dimensions={1,2}, to_apply=%bitcast.152.reduce_sub_computation | reduce | bytes 2097154
  438.8 4.6 reshape.217
  443.4 5.6 all-to-all-start.1
  449.0 8.1 %multiply_reduce_fusion.2 = (f32[3,64]{1,0:T(4,128)S(1)}, f32[3,64]{1,0:T(4,128)S(1)}, f32[8192,3,64]{0,2,1:T(8,128)S(1)}) fusion(f32[8192,3,64]{0,2,1:T(8,128)} %reshape.208, f32[8192]{0:T(1024)S(1)} %get-tuple-element.229, f32[8192,1,64]{0,2,1:T(8,128)S(1)} %slice_multiply_fusion.2, f32[8192,1,64]{0,2,1:T(8,128)} %get-tuple-element.214, ...), kind=kLoop, calls=%fused_computation.33 | loop fusion | flops 12582528 | bytes 18941440 | tf_op jit(solution)/shard_map/reduce_sum | solution.py:179
  457.2 4.8 fusion.13
  462.0 11.2 %copy.82 = bf16[1,8192,3,64]{3,2,0,1:T(4,128)(2,1)} copy(bf16[1,8192,3,64]{1,3,2,0:T(8,128)(2,1)} %fusion.13) | data formatting | bytes 6291456 | tf_op jit(solution)/shard_map/broadcast_in_dim | solution.py:243
  473.2 13.3 %reshape.221 = bf16[64,2,12288]{2,1,0:T(2,128)(2,1)} reshape(bf16[8192,1,3,64]{3,2,1,0:T(4,128)(2,1)} %bitcast.185) | data formatting | bytes 6291456
  486.5 10.7 %all-to-all-start.3 = ((bf16[64,2,12288]{2,1,0:T(2,128)(2,1)}), bf16[64,2,12288]{2,1,0:T(2,128)(2,1)}, u32[]{:S(2)}, u32[]{:S(2)}) async-start(bf16[64,2,12288]{2,1,0:T(2,128)(2,1)} %reshape.221), calls=%async_computation.3 | async-start | bytes 6291456 | tf_op jit(solution)/shard_map/all_to_all | solution.py:243
  497.3 39.8 %while.34 = (s32[]{:T(128)}, f32[16,4,128,256]{3,2,1,0:T(8,128)}, bf16[16,4,128,4,16]{2,1,0,4,3:T(4,128)(2,1)S(1)}, bf16[16,4,256,4,16]{2,4,3,1,0:T(8,128)(2,1)}, s32[16,4,256]{2,1,0:T(4,128)S(1)}, /*index=5*/s32[]{:T(128)}) while((s32[]{:T(128)}, f32[16,4,128,256]{3,2,1,0:T(8,128)}, bf16[16,4,128,4,16]{2,1,0,4,3:T(4,128)(2,1)S(1)}, ...), condition=%wide.region_10.11_spmd, body=%wide.region_8.10_spmd.sunk | while | flops 17956864 | bytes 2967645 | solution.py:127
  545.9 4.8 reduce_sum.66
  560.3 9.5 %all-reduce.8 = (f32[3,3,64]{2,0,1:T(4,128)S(1)}, f32[4,128]{1,0:T(4,128)S(1)}, f32[64]{0:T(128)S(1)}) all-reduce(f32[3,3,64]{2,0,1:T(4,128)S(1)} %pad_maximum_fusion.3, f32[4,128]{1,0:T(4,128)S(1)} %rev.7, f32[64]{0:T(128)S(1)} %get-tuple-element.212), channel_id=1, replica_groups=mesh['seq'=64,'dp'=4] {'dp'}, use_global_device_ids=true, to_apply=%region_7.8 | all-reduce | flops 1152 | bytes 9216 | tf_op jit(solution)/shard_map/psum | solution.py:246
  571.5 10.1 %reshape.218 = bf16[8192,1,1,64]{3,2,1,0:T(2,128)(2,1)} reshape(bf16[64,2,4096]{2,1,0:T(2,128)(2,1)} %all-to-all-done.1) | data formatting | bytes 2097152
  581.6 8.2 %copy.70 = bf16[1,8192,1,64]{1,3,2,0:T(8,128)(2,1)S(1)} copy(bf16[1,8192,1,64]{3,2,0,1:T(2,128)(2,1)} %bitcast.191) | data formatting | bytes 2097152 | tf_op jit(solution)/shard_map/all_to_all | solution.py:242
  592.1 13.1 %reshape.222 = bf16[8192,1,3,64]{3,2,1,0:T(4,128)(2,1)} reshape(bf16[64,2,12288]{2,1,0:T(2,128)(2,1)} %all-to-all-done.3) | data formatting | bytes 6291456
  605.1 10.5 %copy.94 = bf16[1,64,128,3,64]{2,4,1,3,0:T(8,128)(2,1)S(1)} copy(bf16[1,64,128,3,64]{4,3,2,1,0:T(4,128)(2,1)} %bitcast.186) | data formatting | bytes 6291456 | tf_op jit(solution)/shard_map/all_to_all | solution.py:243
  (375 shorter events, 206.7 us)
Async XLA Ops:
  29.7 41.7 %all-to-all-start.2 = ((bf16[64,2,4096]{2,1,0:T(2,128)(2,1)}), bf16[64,2,4096]{2,1,0:T(2,128)(2,1)S(1)}, u32[]{:S(2)}, u32[]{:S(2)}) async-start(bf16[64,2,4096]{2,1,0:T(2,128)(2,1)} %reshape.219), calls=%async_computation.2 | async-start | bytes 2097152 | tf_op jit(solution)/shard_map/all_to_all | solution.py:236
  50.0 27.9 %copy-start.12 = (f32[4,128]{1,0:T(4,128)S(1)}, f32[4,128]{1,0:T(4,128)}, u32[]{:S(2)}) copy-start(f32[4,128]{1,0:T(4,128)} %param.16) | copy-start | bytes 6148
  50.0 28.0 %copy-start.11 = (f32[3,3,64]{2,1,0:T(4,128)S(1)}, f32[3,3,64]{2,1,0:T(4,128)}, u32[]{:S(2)}) copy-start(f32[3,3,64]{2,1,0:T(4,128)} %param.15) | copy-start | bytes 6916
  71.4 141.9 %all-to-all-start = ((bf16[1,128,3,4096]{1,2,0,3:T(4,128)(2,1)}), bf16[1,128,3,4096]{1,2,0,3:T(4,128)(2,1)}, u32[]{:S(2)}, u32[]{:S(2)}) async-start(bf16[1,128,3,4096]{1,2,0,3:T(4,128)(2,1)} %copy.64), calls=%async_computation | async-start | bytes 8388608 | tf_op jit(solution)/shard_map/all_to_all | solution.py:235
  78.1 2.6 copy-start.14
  240.0 5.2 copy-start
  240.0 3.1 copy-start.4
  311.0 3.9 copy-start.8
  366.8 3.1 copy-start.13
  369.9 3.7 copy-start.5
  369.9 3.7 copy-start.6
  370.0 4.5 copy-start.7
  443.4 43.1 %all-to-all-start.1 = ((bf16[64,2,4096]{2,1,0:T(2,128)(2,1)}), bf16[64,2,4096]{2,1,0:T(2,128)(2,1)}, u32[]{:S(2)}, u32[]{:S(2)}) async-start(bf16[64,2,4096]{2,1,0:T(2,128)(2,1)} %reshape.217), calls=%async_computation.1 | async-start | bytes 2097152 | tf_op jit(solution)/shard_map/all_to_all | solution.py:242
  449.0 8.1 %copy-start.9 = (f32[8192]{0:T(1024)S(1)}, f32[8192]{0:T(1024)}, u32[]{:S(2)}) copy-start(f32[8192]{0:T(1024)} %get-tuple-element.227) | copy-start | bytes 98308
  449.0 8.1 %copy-start.10 = (f32[8192]{0:T(1024)S(1)}, f32[8192]{0:T(1024)}, u32[]{:S(2)}) copy-start(f32[8192]{0:T(1024)} %get-tuple-element.230) | copy-start | bytes 98308
  486.5 105.5 %all-to-all-start.3 = ((bf16[64,2,12288]{2,1,0:T(2,128)(2,1)}), bf16[64,2,12288]{2,1,0:T(2,128)(2,1)}, u32[]{:S(2)}, u32[]{:S(2)}) async-start(bf16[64,2,12288]{2,1,0:T(2,128)(2,1)} %reshape.221), calls=%async_computation.3 | async-start | bytes 6291456 | tf_op jit(solution)/shard_map/all_to_all | solution.py:243
  537.4 2.6 copy-start.2
  540.4 2.7 copy-start.1
  550.7 6.3 %copy-start.3 = (bf16[1,128,3,4096]{1,3,2,0:T(8,128)(2,1)S(1)}, bf16[1,128,3,4096]{1,3,2,0:T(8,128)(2,1)}, u32[]{:S(2)}) copy-start(bf16[1,128,3,4096]{1,3,2,0:T(8,128)(2,1)} %get-tuple-element.217) | copy-start | bytes 9437188
where the time goes:
time: 631 us; the launch traced here: 619 us
  local copies, waits for them, and re-layouts  235 us (37%)
  other arithmetic  141 us (22%)
  blocking collectives  133 us (21%)
  matrix products  51.3 us (8%)
  starting transfers between devices  35.8 us (6%)
  waiting for transfers between devices  21.4 us (3%)
    all_gather x1, blocking collectives, local(): all_ids = lax.all_gather(doc_ids, 'seq', axis=1, tiled=True)[0]  123 us
    unnamed x2, other arithmetic  69.1 us
    unnamed x50, local copies, waits for them, and re-layouts  61.9 us
    dot_general x32, matrix products, conv_one_turn(): jnp.einsum('ngts,nsgc->ntgc', masked, data_win, preferred_element_type=jn...  28.4 us
    dynamic_update_slice x32, local copies, waits for them, and re-layouts, conv_blocks(): result = lax.map(conv_one_turn, (data_turns, id_turns, span_index))  24.9 us
    dot_general x16, matrix products, long_one_turn(): jnp.einsum('ntgc,nsgc->ngts', grad_part, data_win, preferred_element_type...  22.9 us
    all_to_all x1, waiting for transfers between devices, local(): lax.all_to_all(cotangent[:, :, None, :], 'seq', split_axis=3, concat_axis...  21.4 us
    dynamic_slice x16, local copies, waits for them, and re-layouts, conv_blocks(): result = lax.map(conv_one_turn, (data_turns, id_turns, span_index))  15.2 us
  transfers between devices with their start and end apart: 4, of which 1 were waited for; matrix products, arithmetic and copies ran while one was open for 23% of the time, Pallas kernels for 0%

commit v1 on v0

v1 whole, which is shorter than its diff:
```python
import functools
import math

import jax
import jax.numpy as jnp
from jax import lax
from jax.experimental import pallas as pl
from jax.experimental.pallas import tpu as pltpu
from jax.sharding import PartitionSpec as P

F32 = jnp.float32
BF16 = jnp.bfloat16
W = 128
PR = 24
CORES = 2


def dot(a, b, dims):
    return lax.dot_general(a, b, (dims, ((), ())), preferred_element_type=F32)


def kernel(
    tiles, chips, dps, scale,
    x_hbm, cot_hbm, ids_ref, short_ref, taps_ref, gain_ref,
    mixed_hbm, grad_hbm, short_out, taps_out, gain_out,
    x, cot, mixed, grad, act, g_own, c_own, g_prev, c_next,
    half, half_in, params, tail, tail_in, idp, idn, edge, edge_in, last,
    part, part_in, block, block_in,
    bmask, fmask, tmask, idx, shift,
    load_sem, half_sem, par_send, par_recv, tail_sem, id_sem,
    g_send, g_recv, c_send, c_recv, e_send, e_recv, r_send, r_recv, b_send, b_recv, out_sem,
):
    per = tiles // chips
    seq = lax.axis_index("seq")
    dp = lax.axis_index("dp")
    chip, core = seq // CORES, lax.rem(seq, CORES)
    n = chips * CORES
    nxt, prv = lax.rem(seq + 1, n), lax.rem(seq + n - 1, n)
    sib = chip * CORES + 1 - core

    def remote(src, dst, send, recv, to, to_dp=None):
        where = {"seq": to} if to_dp is None else {"dp": to_dp, "seq": to}
        return pltpu.make_async_remote_copy(
            src_ref=src, dst_ref=dst, send_sem=send, recv_sem=recv,
            device_id=where, device_id_type=pl.DeviceIdType.MESH,
        )

    def wait_bytes(ref, sem):
        pltpu.make_async_copy(ref, ref, sem).wait()

    load_x = pltpu.make_async_copy(x_hbm, x, load_sem.at[0])
    load_c = pltpu.make_async_copy(cot_hbm, cot, load_sem.at[1])
    load_x.start()
    load_c.start()

    barrier = pltpu.get_barrier_semaphore()

    def greet(to, to_dp=None):
        where = {"seq": to} if to_dp is None else {"dp": to_dp, "seq": to}
        pl.semaphore_signal(barrier, 1, device_id=where, device_id_type=pl.DeviceIdType.MESH)

    greet(nxt)
    greet(prv)
    greet(sib)

    def greet_chip(d, carry):
        greet(lax.rem(chip + d, chips) * CORES + core)
        return carry

    lax.fori_loop(1, chips, greet_chip, 0)

    def greet_dp(d, carry):
        other = lax.rem(dp + d, dps)
        greet(seq, other)
        greet(sib, other)
        return carry

    lax.fori_loop(1, dps, greet_dp, 0)
    pl.semaphore_wait(barrier, 3 + (chips - 1) + 2 * (dps - 1))

    id_to_next = remote(ids_ref, idp, id_sem.at[0], id_sem.at[1], nxt)
    id_to_prev = remote(ids_ref, idn, id_sem.at[2], id_sem.at[3], prv)
    id_to_next.start()
    id_to_prev.start()
    lane = lax.broadcasted_iota(jnp.int32, (16, W), 1)
    row = lax.broadcasted_iota(jnp.int32, (8, W), 0)
    sg = jnp.concatenate(
        [short_ref[...], gain_ref[...], jnp.zeros((6, W // 2), F32)], axis=0
    )
    sg = jnp.where(lane // (W // 2) == core, jnp.concatenate([sg, sg], axis=1), 0.0)
    tp = jnp.where(row // 4 == core, jnp.concatenate([taps_ref[...], taps_ref[...]], axis=0), 0.0)
    for p in range(per):
        half[p, 0:16] = sg
        half[p, 16:24] = tp
    to_sib = remote(half, half_in, half_sem.at[0], half_sem.at[1], sib)
    to_sib.start()

    load_x.wait()
    for i in range(3):
        rows = x[i, W - 16 : W].astype(F32)
        tail[2 * i : 2 * i + 2] = rows[14:16]
    tail[6:8] = jnp.zeros((2, tiles * W), F32)
    tail_to_next = remote(tail, tail_in, tail_sem.at[0], tail_sem.at[1], nxt)
    tail_to_next.start()

    to_sib.wait()
    params[pl.ds(chip * per, per)] = half[...] + half_in[...]

    def send_params(d, carry):
        to = lax.rem(chip + chips + 2 - d, chips)
        to = jnp.where(d == 1, lax.rem(chip + 1, chips), lax.rem(chip + chips + 1 - d, chips))
        mine = params.at[pl.ds(chip * per, per)]
        remote(mine, mine, par_send, par_recv.at[chip], to * CORES + core).start()
        return carry

    lax.fori_loop(1, chips, send_params, 0)

    id_to_next.wait()
    id_to_prev.wait()
    own_row = jnp.broadcast_to(ids_ref[...], (W, W)).astype(F32)
    prev_row = jnp.broadcast_to(jnp.where(seq == 0, -1, idp[...]), (W, W)).astype(F32)
    next_row = jnp.broadcast_to(jnp.where(seq == n - 1, -2, idn[...]), (W, W)).astype(F32)
    own_col, prev_col, next_col = own_row.T, prev_row.T, next_row.T
    s_at = lax.broadcasted_iota(jnp.int32, (W, W), 0)
    t_at = lax.broadcasted_iota(jnp.int32, (W, W), 1)
    same_own = jnp.where((s_at <= t_at) & (own_col == own_row), 1.0, 0.0)
    same_prev = jnp.where((s_at > t_at) & (prev_col == own_row), 1.0, 0.0)
    same_next = jnp.where((s_at > t_at) & (own_col == next_row), 1.0, 0.0)
    bmask[0] = same_own.astype(BF16)
    bmask[1] = same_prev.astype(BF16)
    bmask[2] = same_next.astype(BF16)
    fmask[0] = same_own
    fmask[1] = same_next
    idx[0:8] = prev_col[W - 8 : W]
    idx[8 : W + 8] = own_col
    idx[W + 8 : W + 16] = next_col[0:8]
    mine = idx[8 : W + 8]
    tmask[0] = jnp.where(idx[7 : W + 7] == mine, 1.0, 0.0)
    tmask[1] = jnp.where(idx[6 : W + 6] == mine, 1.0, 0.0)
    tmask[2] = jnp.where(idx[9 : W + 9] == mine, 1.0, 0.0)
    tmask[3] = jnp.where(idx[10 : W + 10] == mine, 1.0, 0.0)
    load_c.wait()
    tail_to_next.wait()

    def forward(i, carry):
        tile = lax.rem((chip + chips - 1) * per + i, tiles)
        owner = tile // per
        lanes = pl.ds(pl.multiple_of(tile * W, W), W)

        @pl.when((lax.rem(tile, per) == 0) & (owner != chip))
        def _():
            wait_bytes(params.at[pl.ds(0, per)], par_recv.at[owner])

        w = params[tile, 0:16]
        m1, m2 = tmask[0], tmask[1]
        for s in range(3):
            now = x[s, :, lanes].astype(F32)
            shift[s, 8 : W + 8] = now
            shift[s, 6:8] = tail_in[2 * s : 2 * s + 2, lanes]
            act[s, :, lanes] = (
                w[3 * s : 3 * s + 1] * now
                + w[3 * s + 1 : 3 * s + 2] * (shift[s, 7 : W + 7] * m1)
                + w[3 * s + 2 : 3 * s + 3] * (shift[s, 6 : W + 6] * m2)
            )
        gated = act[1, :, lanes] * act[2, :, lanes]
        cgrad = cot[:, lanes].astype(F32) * act[0, :, lanes]
        g_own[tile] = gated.astype(BF16).T
        c_own[tile] = cgrad.astype(BF16).T
        remote(g_own.at[tile], g_prev.at[tile], g_send, g_recv.at[tile], nxt).start()
        remote(c_own.at[tile], c_next.at[tile], c_send, c_recv.at[tile], prv).start()
        return carry

    lax.fori_loop(0, tiles, forward, 0)

    shift[:, W + 8 : W + 16] = jnp.zeros((3, 8, W), F32)
    lane_group = lax.broadcasted_iota(jnp.int32, (W, W), 1) // 16
    row8 = lax.broadcasted_iota(jnp.int32, (64, W), 0) % 8

    def backward(i, carry):
        tile = lax.rem(chip * per + i, tiles)
        owner = tile // per
        lanes = pl.ds(pl.multiple_of(tile * W, W), W)
        wait_bytes(g_prev.at[tile], g_recv.at[tile])
        wait_bytes(c_next.at[tile], c_recv.at[tile])
        w = params[tile, 0:16]
        taps = params[tile, 16:24]
        k_own, k_prev, k_next = bmask[0], bmask[1], bmask[2]
        gated = act[1, :, lanes] * act[2, :, lanes]
        g16 = gated.astype(BF16)
        gp, go, co, cn = g_prev[tile], g_own[tile], c_own[tile], c_next[tile]
        cc = jnp.concatenate([co, cn], axis=1)
        gg = jnp.concatenate([gp, go], axis=1)
        conv, back, diag = [], [], []
        for g in range(8):
            spread = jnp.broadcast_to(taps[g : g + 1], (W, W))
            turned = pltpu.roll(spread, 0, 1, stride=1, stride_axis=0).astype(BF16)
            own = turned * k_own
            rows = slice(16 * g, 16 * g + 16)
            conv.append(
                dot(gg[rows], jnp.concatenate([turned * k_prev, own], axis=0), ((1,), (0,)))
            )
            back.append(
                dot(cc[rows], jnp.concatenate([own, turned * k_next], axis=1), ((1,), (1,)))
            )
            pair = dot(jnp.where(lane_group == g, g16, jnp.zeros_like(g16)), cc, ((1,), (0,)))
            pair = pair[:, :W] * fmask[0] + pair[:, W:] * fmask[1]
            total = pair[0:8]
            for q in range(1, W // 8):
                total = total + pltpu.roll(pair[8 * q : 8 * q + 8], W - 8 * q, 1)
            diag.append(total)
        diag = jnp.concatenate(diag, axis=0)
        for bit in (1, 2, 4):
            diag = jnp.where((row8 & bit) != 0, pltpu.roll(diag, W - bit, 1), diag)
        part[tile, 16:24] = jnp.sum(diag.reshape(8, 8, W), axis=1)

        gain = w[9:10]
        q_act, k_act, v_act = act[0, :, lanes], act[1, :, lanes], act[2, :, lanes]
        cotan = cot[:, lanes].astype(F32)
        cgrad = cotan * q_act
        convolved = jnp.concatenate(conv, axis=0).T + gain * gated
        mixed[:, lanes] = (q_act * convolved).astype(BF16)
        ggrad = jnp.concatenate(back, axis=0).T + gain * cgrad
        u1, u2 = tmask[2], tmask[3]
        sums = []
        for s, ag in enumerate((cotan * convolved, ggrad * v_act, ggrad * k_act)):
            shift[s, 8 : W + 8] = ag
            edge[tile, 2 * s : 2 * s + 2] = ag[0:2]
            b1 = shift[s, 9 : W + 9] * u1
            b2 = shift[s, 10 : W + 10] * u2
            sgrad = w[3 * s : 3 * s + 1] * ag + w[3 * s + 1 : 3 * s + 2] * b1 + w[3 * s + 2 : 3 * s + 3] * b2
            grad[s, :, lanes] = sgrad.astype(BF16)
            last[s, :, lanes] = sgrad[W - 16 :]
            now = x[s, :, lanes].astype(F32)
            before = tail_in[2 * s : 2 * s + 2, lanes]
            a1 = ag[0:2] * tmask[0, 0:2]
            a2 = ag[0:2] * tmask[1, 0:2]
            sums.append(jnp.sum(now * ag, axis=0, keepdims=True))
            sums.append(jnp.sum(now * b1, axis=0, keepdims=True) + a1[0:1] * before[1:2])
            sums.append(
                jnp.sum(now * b2, axis=0, keepdims=True) + a2[0:1] * before[0:1] + a2[1:2] * before[1:2]
            )
        sums.append(jnp.sum(cgrad * gated, axis=0, keepdims=True))
        sums.append(jnp.zeros((6, W), F32))
        part[tile, 0:16] = jnp.concatenate(sums, axis=0)
        edge[tile, 6:8] = jnp.zeros((2, W), F32)
        remote(edge.at[tile], edge_in.at[tile], e_send, e_recv, prv).start()

        @pl.when(owner != chip)
        def _():
            slot = part_in.at[lax.rem(tile, per), lax.rem(chip + chips - owner, chips) - 1]
            remote(part.at[tile], slot, r_send, r_recv, owner * CORES + core).start()

        pltpu.make_async_copy(mixed.at[:, lanes], mixed_hbm.at[:, lanes], out_sem.at[0]).start()
        pltpu.make_async_copy(
            grad.at[:, 0 : W - 16, lanes], grad_hbm.at[:, 0 : W - 16, lanes], out_sem.at[1]
        ).start()
        return carry

    lax.fori_loop(0, tiles, backward, 0)

    wait_bytes(part_in, r_recv)
    for p in range(per):
        total = part[chip * per + p]
        for d in range(chips - 1):
            total = total + part_in[p, d]
        block[p] = total

    def send_block(d, carry):
        to_dp = lax.rem(dp + d // CORES, dps)
        to = chip * CORES + lax.rem(core + d, CORES)
        remote(block, block_in.at[d - 1], b_send, b_recv, to, to_dp).start()
        return carry

    lax.fori_loop(1, CORES * dps, send_block, 0)

    wait_bytes(edge_in, e_recv)
    zero14 = jnp.zeros((14, W), F32)

    def finish(tile, carry):
        lanes = pl.ds(pl.multiple_of(tile * W, W), W)
        w = params[tile, 0:16]
        for s in range(3):
            e0 = edge_in[tile, 2 * s : 2 * s + 1]
            e1 = edge_in[tile, 2 * s + 1 : 2 * s + 2]
            w1, w2 = w[3 * s + 1 : 3 * s + 2], w[3 * s + 2 : 3 * s + 3]
            r0 = w2 * (e0 * tmask[3, W - 2 : W - 1])
            r1 = w1 * (e0 * tmask[2, W - 1 : W]) + w2 * (e1 * tmask[3, W - 1 : W])
            more = jnp.concatenate([zero14, r0, r1], axis=0)
            grad[s, W - 16 : W, lanes] = (last[s, :, lanes] + more).astype(BF16)
        return carry

    lax.fori_loop(0, tiles, finish, 0)
    rest = pltpu.make_async_copy(
        grad.at[:, W - 16 : W], grad_hbm.at[:, W - 16 : W], out_sem.at[2]
    )
    rest.start()

    wait_bytes(block_in, b_recv)
    total = block[0]
    for d in range(CORES * dps - 1):
        total = total + block_in[d, 0]
    total = total * scale
    top, low = total[0:16], total[16:24]
    top = jnp.where(core == 0, top, pltpu.roll(top, W // 2, 1))
    short_out[...] = top[0:9, : W // 2]
    gain_out[...] = top[9:10, : W // 2]
    taps_out[...] = jnp.where(core == 0, low[0:4], low[4:8])

    wait_bytes(params.at[pl.ds(0, (chips - 1) * per)], par_send)
    wait_bytes(g_own, g_send)
    wait_bytes(c_own, c_send)
    wait_bytes(edge, e_send)
    wait_bytes(part.at[pl.ds(0, (chips - 1) * per)], r_send)
    wait_bytes(block_in, b_send)
    wait_bytes(mixed, out_sem.at[0])
    wait_bytes(grad.at[:, 0 : W - 16], out_sem.at[1])
    rest.wait()


def local(streams, cotangent, doc_ids, short_taps, long_taps, skip_gain):
    channels = cotangent.shape[2]
    n, dps = lax.axis_size("seq"), lax.axis_size("dp")
    tiles, chips = channels // W, n // CORES
    per = tiles // chips
    x = jnp.transpose(streams[0], (1, 0, 2))
    scale = 1.0 / math.sqrt(dps * n * W)
    dma, vmem = pltpu.SemaphoreType.DMA, pltpu.VMEM
    any_, inv = pl.BlockSpec(memory_space=pl.ANY), pl.BlockSpec(memory_space=pltpu.VMEM)
    mixed, grad, short_grad, taps_grad, gain_grad = pl.pallas_call(
        functools.partial(kernel, tiles, chips, dps, scale),
        out_shape=(
            jax.ShapeDtypeStruct((W, channels), BF16),
            jax.ShapeDtypeStruct((3, W, channels), BF16),
            jax.ShapeDtypeStruct((9, W // 2), F32),
            jax.ShapeDtypeStruct((4, W), F32),
            jax.ShapeDtypeStruct((1, W // 2), F32),
        ),
        in_specs=[any_, any_, inv, inv, inv, inv],
        out_specs=(any_, any_, inv, inv, inv),
        scratch_shapes=[
            vmem((3, W, channels), BF16),
            vmem((W, channels), BF16),
            vmem((W, channels), BF16),
            vmem((3, W, channels), BF16),
            vmem((3, W, channels), F32),
            vmem((tiles, W, W), BF16),
            vmem((tiles, W, W), BF16),
            vmem((tiles, W, W), BF16),
            vmem((tiles, W, W), BF16),
            vmem((per, PR, W), F32),
            vmem((per, PR, W), F32),
            vmem((tiles, PR, W), F32),
            vmem((8, channels), F32),
            vmem((8, channels), F32),
            vmem((1, W), jnp.int32),
            vmem((1, W), jnp.int32),
            vmem((tiles, 8, W), F32),
            vmem((tiles, 8, W), F32),
            vmem((3, 16, channels), F32),
            vmem((tiles, PR, W), F32),
            vmem((per, chips - 1, PR, W), F32),
            vmem((per, PR, W), F32),
            vmem((CORES * dps - 1, per, PR, W), F32),
            vmem((3, W, W), BF16),
            vmem((2, W, W), F32),
            vmem((4, W, W), F32),
            vmem((W + 16, W), F32),
            vmem((3, W + 16, W), F32),
            dma((2,)),
            dma((2,)),
            dma(()),
            dma((chips,)),
            dma((2,)),
            dma((4,)),
            dma(()),
            dma((tiles,)),
            dma(()),
            dma((tiles,)),
            dma(()),
            dma(()),
            dma(()),
            dma(()),
            dma(()),
            dma(()),
            dma((3,)),
        ],
        compiler_params=pltpu.CompilerParams(
            collective_id=0, has_side_effects=True, vmem_limit_bytes=48 * 1024 * 1024
        ),
        cost_estimate=pl.CostEstimate(
            flops=6 * W * W * channels, bytes_accessed=16 * W * channels, transcendentals=0
        ),
        name="hyena_block",
    )(
        x,
        cotangent[0],
        doc_ids,
        short_taps.reshape(9, -1)[:, : W // 2],
        long_taps[:4],
        skip_gain.reshape(1, -1)[:, : W // 2],
    )
    return (
        mixed[None],
        jnp.transpose(grad, (1, 0, 2))[None],
        short_grad.reshape(3, 3, W // 2),
        taps_grad,
        gain_grad.reshape(W // 2),
    )


def solution(mesh):
    return jax.shard_map(
        local,
        mesh=mesh,
        in_specs=(
            P("dp", "seq", None, None),
            P("dp", "seq", None),
            P("dp", "seq"),
            P(None, None, "seq"),
            P("seq", None),
            P("seq"),
        ),
        out_specs=(
            P("dp", "seq", None),
            P("dp", "seq", None, None),
            P(None, None, "seq"),
            P("seq", None),
            P("seq"),
        ),
        check_vma=False,
    )
```

time: 631 us -> 79.1 us (0.13); the launches traced: 619 us -> 78.9 us
  local copies, waits for them, and re-layouts: 235 us -> 10.5 us
  other arithmetic: 141 us -> 0 us
  blocking collectives: 133 us -> 0 us
  Pallas kernels: 0 us -> 67.7 us
  matrix products: 51.3 us -> 0 us
  starting transfers between devices: 35.8 us -> 0 us
  waiting for transfers between devices: 21.4 us -> 0 us
    all_gather x1 -> x0, blocking collectives: 123 us -> none  [local(): all_ids = lax.all_gather(doc_ids, 'seq', axis=1, tiled=True)[0]]
    unnamed x2 -> x0, other arithmetic: 69.1 us -> none
    pallas_call x0 -> x1, Pallas kernels: none -> 67.7 us  [local(): pl.pallas_call(functools.partial(kernel, tiles, chips, dps, scale), out_s...]
    unnamed x50 -> x14, local copies, waits for them, and re-layouts: 61.9 us -> 9.22 us
    dot_general x48 -> x0, matrix products: 51.3 us -> none  [the longest x32 28.4 us: conv_one_turn(): jnp.einsum('ngts,nsgc->ntgc', masked, data_win, preferred_element_type=jn...]
    dynamic_update_slice x48 -> x0, local copies, waits for them, and re-layouts: 38.6 us -> none  [the longest x32 24.9 us: conv_blocks(): result = lax.map(conv_one_turn, (data_turns, id_turns, span_index))]
    all_to_all x4 -> x0, starting transfers between devices: 35.8 us -> none  [the longest x1 13.2 us: local(): lax.all_to_all(cotangent[:, :, None, :], 'seq', split_axis=3, concat_axis...]
    convert_element_type x6 -> x0, local copies, waits for them, and re-layouts: 30.2 us -> none  [the longest x2 13.4 us: one_sequence(): streams.astype(jnp.float32)]
  transfers between devices with their start and end apart: 4 -> 0, of which waited for: 1 -> 0; matrix products, arithmetic and copies ran while one was open for 23% -> 0% of each run, Pallas kernels for 0% -> 0%
where the time goes in v1:
time: 79.1 us; the launch traced here: 78.9 us
  Pallas kernels  67.7 us (86%)
  local copies, waits for them, and re-layouts  10.5 us (13%)
    pallas_call x1, Pallas kernels, local(): pl.pallas_call(functools.partial(kernel, tiles, chips, dps, scale), out_s...  67.7 us
    unnamed x14, local copies, waits for them, and re-layouts  9.22 us

profile of v1, /device:TPU:1, one launch (start us, length us, event | category | flops | bytes accessed | tf_op | source)
XLA Modules:
  0.0 78.9 jit_solution(2571603159654691910)
XLA Ops:
  0.6 0.7 reshape.22.short_ref
  1.3 0.0 copy-start.1
  1.3 1.2 %copy-done.1 = bf16[1,128,4096]{2,1,0:T(8,128)(2,1)S(1)} copy-done((bf16[1,128,4096]{2,1,0:T(8,128)(2,1)S(1)}, bf16[1,128,4096]{2,1,0:T(8,128)(2,1)}, u32[]{:S(2)}) %copy-start.1) | copy-done | bytes 1048600
  2.6 0.0 copy-start.2
  2.6 0.7 copy-done.2
  3.2 0.0 copy-start.3
  3.2 0.7 copy-done.3
  3.9 0.0 copy-start.4
  3.9 0.7 copy-done.4
  4.5 67.7 %hyena_block.1 = (bf16[128,4096]{1,0:T(8,128)(2,1)S(1)}, bf16[3,128,4096]{2,1,0:T(8,128)(2,1)S(1)}, f32[9,64]{1,0:T(8,128)S(1)}, f32[4,128]{1,0:T(4,128)S(1)}, f32[1,64]{1,0:T(1,128)S(1)}) custom-call(bf16[3,128,4096]{2,1,0:T(8,128)(2,1)} %bitcast.15, bf16[128,4096]{1,0:T(8,128)(2,1)S(1)} %bitcast.12, s32[1,128]{1,0:T(1,128)S(1)} %copy-done.3, ...), custom_call_target="tpu_custom_call" | custom-call | flops 402653184 | bytes 8388608 | tf_op jit(solution)/shard_map/hyena_block/pallas_call | solution.py:329
  72.3 0.0 copy-start
  72.3 1.0 %copy-done = bf16[128,4096]{1,0:T(8,128)(2,1)} copy-done((bf16[128,4096]{1,0:T(8,128)(2,1)}, bf16[128,4096]{1,0:T(8,128)(2,1)S(1)}, u32[]{:S(2)}) %copy-start) | copy-done | bytes 1048600
  73.2 0.6 reshape.24
  73.8 2.3 %copy.15 = bf16[1,128,4096]{2,1,0:T(8,128)(2,1)} copy(bf16[1,128,4096]{2,1,0:T(8,128)(2,1)} %bitcast.11) | data formatting | bytes 2097152
  76.1 1.7 %copy.16 = bf16[1,128,3,4096]{3,1,2,0:T(8,128)(2,1)} copy(bf16[1,128,3,4096]{3,1,2,0:T(8,128)(2,1)S(1)} %bitcast.10) | data formatting | bytes 6291456
  77.8 0.6 copy.17
  78.4 0.5 copy.18
Async XLA Ops:
  1.3 1.2 %copy-start.1 = (bf16[1,128,4096]{2,1,0:T(8,128)(2,1)S(1)}, bf16[1,128,4096]{2,1,0:T(8,128)(2,1)}, u32[]{:S(2)}) copy-start(bf16[1,128,4096]{2,1,0:T(8,128)(2,1)} %param.7) | copy-start | bytes 3145732
  2.6 0.7 copy-start.2
  3.2 0.7 copy-start.3
  3.9 0.7 copy-start.4
  72.3 1.0 %copy-start = (bf16[128,4096]{1,0:T(8,128)(2,1)}, bf16[128,4096]{1,0:T(8,128)(2,1)S(1)}, u32[]{:S(2)}) copy-start(bf16[128,4096]{1,0:T(8,128)(2,1)S(1)} %get-tuple-element.10) | copy-start | bytes 3145732

commit v2 on v1

--- a/solution.py
+++ b/solution.py
@@ -11,7 +11,7 @@
 F32 = jnp.float32
 BF16 = jnp.bfloat16
 W = 128
-PR = 24
+PR = 18
 CORES = 2
 
 
@@ -21,14 +21,14 @@
 
 def kernel(
     tiles, chips, dps, scale,
-    x_hbm, cot_hbm, ids_ref, short_ref, taps_ref, gain_ref,
-    mixed_hbm, grad_hbm, short_out, taps_out, gain_out,
-    x, cot, mixed, grad, act, g_own, c_own, g_prev, c_next,
+    x_hbm, cot_hbm, ids_hbm, short_hbm, taps_hbm, gain_hbm,
+    out, small_out,
+    x, cot, ids_ref, short_ref, taps_ref, gain_ref, act, g_own, c_own, g_prev, c_next,
     half, half_in, params, tail, tail_in, idp, idn, edge, edge_in, last,
     part, part_in, block, block_in,
-    bmask, fmask, tmask, idx, shift,
-    load_sem, half_sem, par_send, par_recv, tail_sem, id_sem,
-    g_send, g_recv, c_send, c_recv, e_send, e_recv, r_send, r_recv, b_send, b_recv, out_sem,
+    bmask, perm, turn, rtaps, tmask, idx, shift,
+    load_sem, half_sem, par_send, par_pass, par_recv, tail_sem, id_sem,
+    g_send, g_recv, c_send, c_recv, e_send, e_recv, r_send, r_recv, b_send, b_recv,
 ):
     per = tiles // chips
     seq = lax.axis_index("seq")
@@ -50,8 +50,18 @@
 
     load_x = pltpu.make_async_copy(x_hbm, x, load_sem.at[0])
     load_c = pltpu.make_async_copy(cot_hbm, cot, load_sem.at[1])
+    small = [
+        pltpu.make_async_copy(a, b, load_sem.at[2 + q])
+        for q, (a, b) in enumerate(
+            ((ids_hbm, ids_ref), (short_hbm, short_ref), (taps_hbm, taps_ref), (gain_hbm, gain_ref))
+        )
+    ]
+    for copy in small:
+        copy.start()
     load_x.start()
     load_c.start()
+    peers = dps * CORES
+    place = dp * CORES + core
 
     barrier = pltpu.get_barrier_semaphore()
 
@@ -78,20 +88,21 @@
     lax.fori_loop(1, dps, greet_dp, 0)
     pl.semaphore_wait(barrier, 3 + (chips - 1) + 2 * (dps - 1))
 
+    for copy in small:
+        copy.wait()
     id_to_next = remote(ids_ref, idp, id_sem.at[0], id_sem.at[1], nxt)
     id_to_prev = remote(ids_ref, idn, id_sem.at[2], id_sem.at[3], prv)
     id_to_next.start()
     id_to_prev.start()
-    lane = lax.broadcasted_iota(jnp.int32, (16, W), 1)
+    lane = lax.broadcasted_iota(jnp.int32, (10, W), 1)
     row = lax.broadcasted_iota(jnp.int32, (8, W), 0)
-    sg = jnp.concatenate(
-        [short_ref[...], gain_ref[...], jnp.zeros((6, W // 2), F32)], axis=0
-    )
+    sg = jnp.concatenate([short_ref[0], short_ref[1], short_ref[2], gain_ref[...]], axis=0)[:, : W // 2]
     sg = jnp.where(lane // (W // 2) == core, jnp.concatenate([sg, sg], axis=1), 0.0)
-    tp = jnp.where(row // 4 == core, jnp.concatenate([taps_ref[...], taps_ref[...]], axis=0), 0.0)
+    tp = taps_ref[0:4]
+    tp = jnp.where(row // 4 == core, jnp.concatenate([tp, tp], axis=0), 0.0)
     for p in range(per):
-        half[p, 0:16] = sg
-        half[p, 16:24] = tp
+        half[p, 0:10] = sg
+        half[p, 10:18] = tp
     to_sib = remote(half, half_in, half_sem.at[0], half_sem.at[1], sib)
     to_sib.start()
 
@@ -106,14 +117,39 @@
     to_sib.wait()
     params[pl.ds(chip * per, per)] = half[...] + half_in[...]
 
-    def send_params(d, carry):
-        to = lax.rem(chip + chips + 2 - d, chips)
-        to = jnp.where(d == 1, lax.rem(chip + 1, chips), lax.rem(chip + chips + 1 - d, chips))
+    rounds = -(-chips // peers)
+
+    def each_round(act_on):
+        def body(m, carry):
+            d = place + peers * m
+
+            @pl.when((d > 0) & (d < chips))
+            def _():
+                act_on(d)
+
+            return carry
+
+        lax.fori_loop(0, rounds, body, 0)
+
+    def send_params(d):
         mine = params.at[pl.ds(chip * per, per)]
-        remote(mine, mine, par_send, par_recv.at[chip], to * CORES + core).start()
-        return carry
-
-    lax.fori_loop(1, chips, send_params, 0)
+        to = lax.rem(chip + d, chips) * CORES + core
+        remote(mine, mine, par_send.at[d], par_recv.at[chip], to).start()
+
+    def pass_params(d):
+        source = lax.rem(chip + chips - d, chips)
+        mine = params.at[pl.ds(source * per, per)]
+        wait_bytes(mine, par_recv.at[source])
+
+        def one(e, carry):
+            peer = lax.rem(place + e, peers)
+            to = chip * CORES + lax.rem(peer, CORES)
+            remote(mine, mine, par_pass.at[d], par_recv.at[source], to, peer // CORES).start()
+            return carry
+
+        lax.fori_loop(1, peers, one, 0)
+
+    each_round(send_params)
 
     id_to_next.wait()
     id_to_prev.wait()
@@ -129,8 +165,13 @@
     bmask[0] = same_own.astype(BF16)
     bmask[1] = same_prev.astype(BF16)
     bmask[2] = same_next.astype(BF16)
-    fmask[0] = same_own
-    fmask[1] = same_next
+    bmask[3] = same_own.T.astype(BF16)
+    bmask[4] = same_next.T.astype(BF16)
+    turn[...] = jnp.where((s_at + t_at) % W == 0, 1.0, 0.0).astype(BF16)
+    for q in range(8):
+        perm[q * W : q * W + W] = jnp.where(
+            (s_at + t_at + 1 - 16 * q) % W == 0, 1.0, 0.0
+        ).astype(BF16)
     idx[0:8] = prev_col[W - 8 : W]
     idx[8 : W + 8] = own_col
     idx[W + 8 : W + 16] = next_col[0:8]
@@ -139,6 +180,7 @@
     tmask[1] = jnp.where(idx[6 : W + 6] == mine, 1.0, 0.0)
     tmask[2] = jnp.where(idx[9 : W + 9] == mine, 1.0, 0.0)
     tmask[3] = jnp.where(idx[10 : W + 10] == mine, 1.0, 0.0)
+    each_round(pass_params)
     load_c.wait()
     tail_to_next.wait()
 
@@ -147,11 +189,14 @@
         owner = tile // per
         lanes = pl.ds(pl.multiple_of(tile * W, W), W)
 
-        @pl.when((lax.rem(tile, per) == 0) & (owner != chip))
+        far = lax.rem(chip + chips - owner, chips)
+
+        @pl.when((lax.rem(tile, per) == 0) & (lax.rem(far, peers) != place) & (far != 0))
         def _():
             wait_bytes(params.at[pl.ds(0, per)], par_recv.at[owner])
 
-        w = params[tile, 0:16]
+        w = params[tile, 0:10]
+        rtaps[tile] = dot(params[tile, 10:18].astype(BF16), turn[...], ((1,), (0,)))
         m1, m2 = tmask[0], tmask[1]
         for s in range(3):
             now = x[s, :, lanes].astype(F32)
@@ -174,7 +219,10 @@
 
     shift[:, W + 8 : W + 16] = jnp.zeros((3, 8, W), F32)
     lane_group = lax.broadcasted_iota(jnp.int32, (W, W), 1) // 16
-    row8 = lax.broadcasted_iota(jnp.int32, (64, W), 0) % 8
+
+    def circulant(row):
+        spread = jnp.broadcast_to(row, (W, W))
+        return pltpu.roll(spread, 0, 1, stride=1, stride_axis=0).astype(BF16)
 
     def backward(i, carry):
         tile = lax.rem(chip * per + i, tiles)
@@ -182,43 +230,51 @@
         lanes = pl.ds(pl.multiple_of(tile * W, W), W)
         wait_bytes(g_prev.at[tile], g_recv.at[tile])
         wait_bytes(c_next.at[tile], c_recv.at[tile])
-        w = params[tile, 0:16]
-        taps = params[tile, 16:24]
-        k_own, k_prev, k_next = bmask[0], bmask[1], bmask[2]
+        w = params[tile, 0:10]
+        taps = params[tile, 10:18]
+        flipped = rtaps[tile]
+        k_own, k_prev, k_next, o_own, o_next = [bmask[q] for q in range(5)]
         gated = act[1, :, lanes] * act[2, :, lanes]
         g16 = gated.astype(BF16)
-        gp, go, co, cn = g_prev[tile], g_own[tile], c_own[tile], c_next[tile]
-        cc = jnp.concatenate([co, cn], axis=1)
-        gg = jnp.concatenate([gp, go], axis=1)
-        conv, back, diag = [], [], []
+        cc = jnp.concatenate([c_own[tile], c_next[tile]], axis=1)
+        gg = jnp.concatenate([g_prev[tile], g_own[tile]], axis=1)
+        conv, back, pairs = [], [], []
         for g in range(8):
-            spread = jnp.broadcast_to(taps[g : g + 1], (W, W))
-            turned = pltpu.roll(spread, 0, 1, stride=1, stride_axis=0).astype(BF16)
-            own = turned * k_own
+            fwd = circulant(taps[g : g + 1])
+            rev = circulant(flipped[g : g + 1])
             rows = slice(16 * g, 16 * g + 16)
             conv.append(
-                dot(gg[rows], jnp.concatenate([turned * k_prev, own], axis=0), ((1,), (0,)))
+                dot(gg[rows], jnp.concatenate([fwd * k_prev, fwd * k_own], axis=0), ((1,), (0,)))
             )
             back.append(
-                dot(cc[rows], jnp.concatenate([own, turned * k_next], axis=1), ((1,), (1,)))
+                dot(cc[rows], jnp.concatenate([rev * o_own, rev * o_next], axis=0), ((1,), (0,)))
             )
             pair = dot(jnp.where(lane_group == g, g16, jnp.zeros_like(g16)), cc, ((1,), (0,)))
-            pair = pair[:, :W] * fmask[0] + pair[:, W:] * fmask[1]
-            total = pair[0:8]
-            for q in range(1, W // 8):
-                total = total + pltpu.roll(pair[8 * q : 8 * q + 8], W - 8 * q, 1)
-            diag.append(total)
-        diag = jnp.concatenate(diag, axis=0)
-        for bit in (1, 2, 4):
-            diag = jnp.where((row8 & bit) != 0, pltpu.roll(diag, W - bit, 1), diag)
-        part[tile, 16:24] = jnp.sum(diag.reshape(8, 8, W), axis=1)
+            pair = pair.astype(BF16)
+            pairs.append(pair[:, :W] * k_own + pair[:, W:] * k_next)
+        lined = jnp.concatenate(
+            [
+                jnp.concatenate([pair[16 * q : 16 * q + 16] for pair in pairs], axis=0)
+                for q in range(8)
+            ],
+            axis=1,
+        )
+        diag = dot(lined, perm[...], ((1,), (0,)))
+        diag = [
+            jnp.sum(
+                pltpu.roll(diag[16 * g : 16 * g + 16], 0, 1, stride=1, stride_axis=0),
+                axis=0, keepdims=True,
+            )
+            for g in range(8)
+        ]
+        part[tile, 10:18] = jnp.concatenate(diag, axis=0)
 
         gain = w[9:10]
         q_act, k_act, v_act = act[0, :, lanes], act[1, :, lanes], act[2, :, lanes]
         cotan = cot[:, lanes].astype(F32)
         cgrad = cotan * q_act
         convolved = jnp.concatenate(conv, axis=0).T + gain * gated
-        mixed[:, lanes] = (q_act * convolved).astype(BF16)
+        out[0, :, lanes] = (q_act * convolved).astype(BF16)
         ggrad = jnp.concatenate(back, axis=0).T + gain * cgrad
         u1, u2 = tmask[2], tmask[3]
         sums = []
@@ -228,7 +284,7 @@
             b1 = shift[s, 9 : W + 9] * u1
             b2 = shift[s, 10 : W + 10] * u2
             sgrad = w[3 * s : 3 * s + 1] * ag + w[3 * s + 1 : 3 * s + 2] * b1 + w[3 * s + 2 : 3 * s + 3] * b2
-            grad[s, :, lanes] = sgrad.astype(BF16)
+            out[s + 1, :, lanes] = sgrad.astype(BF16)
             last[s, :, lanes] = sgrad[W - 16 :]
             now = x[s, :, lanes].astype(F32)
             before = tail_in[2 * s : 2 * s + 2, lanes]
@@ -240,8 +296,7 @@
                 jnp.sum(now * b2, axis=0, keepdims=True) + a2[0:1] * before[0:1] + a2[1:2] * before[1:2]
             )
         sums.append(jnp.sum(cgrad * gated, axis=0, keepdims=True))
-        sums.append(jnp.zeros((6, W), F32))
-        part[tile, 0:16] = jnp.concatenate(sums, axis=0)
+        part[tile, 0:10] = jnp.concatenate(sums, axis=0)
         edge[tile, 6:8] = jnp.zeros((2, W), F32)
         remote(edge.at[tile], edge_in.at[tile], e_send, e_recv, prv).start()
 
@@ -250,10 +305,6 @@
             slot = part_in.at[lax.rem(tile, per), lax.rem(chip + chips - owner, chips) - 1]
             remote(part.at[tile], slot, r_send, r_recv, owner * CORES + core).start()
 
-        pltpu.make_async_copy(mixed.at[:, lanes], mixed_hbm.at[:, lanes], out_sem.at[0]).start()
-        pltpu.make_async_copy(
-            grad.at[:, 0 : W - 16, lanes], grad_hbm.at[:, 0 : W - 16, lanes], out_sem.at[1]
-        ).start()
         return carry
 
     lax.fori_loop(0, tiles, backward, 0)
@@ -278,7 +329,7 @@
 
     def finish(tile, carry):
         lanes = pl.ds(pl.multiple_of(tile * W, W), W)
-        w = params[tile, 0:16]
+        w = params[tile, 0:10]
         for s in range(3):
             e0 = edge_in[tile, 2 * s : 2 * s + 1]
             e1 = edge_in[tile, 2 * s + 1 : 2 * s + 2]
@@ -286,35 +337,50 @@
             r0 = w2 * (e0 * tmask[3, W - 2 : W - 1])
             r1 = w1 * (e0 * tmask[2, W - 1 : W]) + w2 * (e1 * tmask[3, W - 1 : W])
             more = jnp.concatenate([zero14, r0, r1], axis=0)
-            grad[s, W - 16 : W, lanes] = (last[s, :, lanes] + more).astype(BF16)
+            out[s + 1, W - 16 : W, lanes] = (last[s, :, lanes] + more).astype(BF16)
         return carry
 
     lax.fori_loop(0, tiles, finish, 0)
-    rest = pltpu.make_async_copy(
-        grad.at[:, W - 16 : W], grad_hbm.at[:, W - 16 : W], out_sem.at[2]
-    )
-    rest.start()
-
     wait_bytes(block_in, b_recv)
     total = block[0]
     for d in range(CORES * dps - 1):
         total = total + block_in[d, 0]
     total = total * scale
-    top, low = total[0:16], total[16:24]
-    top = jnp.where(core == 0, top, pltpu.roll(top, W // 2, 1))
-    short_out[...] = top[0:9, : W // 2]
-    gain_out[...] = top[9:10, : W // 2]
-    taps_out[...] = jnp.where(core == 0, low[0:4], low[4:8])
-
-    wait_bytes(params.at[pl.ds(0, (chips - 1) * per)], par_send)
+    top, low = total[0:10], total[10:18]
+    small_out[0:10] = jnp.where(core == 0, top, pltpu.roll(top, W // 2, 1))
+    small_out[16:20] = jnp.where(core == 0, low[0:4], low[4:8])
+    small_out[20:24] = jnp.zeros((4, W), F32)
+
+    def sent_params(d):
+        wait_bytes(params.at[pl.ds(0, per)], par_send.at[d])
+        wait_bytes(block_in, par_pass.at[d])
+
+    each_round(sent_params)
     wait_bytes(g_own, g_send)
     wait_bytes(c_own, c_send)
     wait_bytes(edge, e_send)
     wait_bytes(part.at[pl.ds(0, (chips - 1) * per)], r_send)
     wait_bytes(block_in, b_send)
-    wait_bytes(mixed, out_sem.at[0])
-    wait_bytes(grad.at[:, 0 : W - 16], out_sem.at[1])
-    rest.wait()
+
+
+def hand_over(out, small, mixed, grad, short_grad, taps_grad, gain_grad, sem):
+    copies = [pltpu.make_async_copy(out.at[0], mixed, sem.at[0])]
+    for s in range(3):
+        copies.append(pltpu.make_async_copy(out.at[s + 1], grad.at[s], sem.at[s + 1]))
+    for copy in copies:
+        copy.start()
+    for s in range(3):
+        short_grad[s] = small[3 * s : 3 * s + 3, : W // 2]
+    gain_grad[...] = small[9:10, : W // 2]
+    s_at = lax.broadcasted_iota(jnp.int32, (W, W), 0)
+    t_at = lax.broadcasted_iota(jnp.int32, (W, W), 1)
+    flip = jnp.where(s_at + t_at == W - 1, 1.0, 0.0)
+    taps_grad[...] = lax.dot_general(
+        small[16:24], flip, (((1,), (0,)), ((), ())),
+        precision=lax.Precision.HIGHEST, preferred_element_type=F32,
+    )[0:4]
+    for copy in copies:
+        copy.wait()
 
 
 def local(streams, cotangent, doc_ids, short_taps, long_taps, skip_gain):
@@ -325,23 +391,22 @@
     x = jnp.transpose(streams[0], (1, 0, 2))
     scale = 1.0 / math.sqrt(dps * n * W)
     dma, vmem = pltpu.SemaphoreType.DMA, pltpu.VMEM
-    any_, inv = pl.BlockSpec(memory_space=pl.ANY), pl.BlockSpec(memory_space=pltpu.VMEM)
-    mixed, grad, short_grad, taps_grad, gain_grad = pl.pallas_call(
+    any_, inv = pl.BlockSpec(memory_space=pltpu.HBM), pl.BlockSpec(memory_space=pltpu.VMEM)
+    out, small = pl.pallas_call(
         functools.partial(kernel, tiles, chips, dps, scale),
         out_shape=(
-            jax.ShapeDtypeStruct((W, channels), BF16),
-            jax.ShapeDtypeStruct((3, W, channels), BF16),
-            jax.ShapeDtypeStruct((9, W // 2), F32),
-            jax.ShapeDtypeStruct((4, W), F32),
-            jax.ShapeDtypeStruct((1, W // 2), F32),
+            jax.ShapeDtypeStruct((4, W, channels), BF16),
+            jax.ShapeDtypeStruct((24, W), F32),
         ),
-        in_specs=[any_, any_, inv, inv, inv, inv],
-        out_specs=(any_, any_, inv, inv, inv),
+        in_specs=[any_] * 6,
+        out_specs=(inv, inv),
         scratch_shapes=[
             vmem((3, W, channels), BF16),
             vmem((W, channels), BF16),
-            vmem((W, channels), BF16),
-            vmem((3, W, channels), BF16),
+            vmem(doc_ids.shape, jnp.int32),
+            vmem(short_taps.shape, F32),
+            vmem(long_taps.shape, F32),
+            vmem((1,) + skip_gain.shape, F32),
             vmem((3, W, channels), F32),
             vmem((tiles, W, W), BF16),
             vmem((tiles, W, W), BF16),
@@ -361,14 +426,17 @@
             vmem((per, chips - 1, PR, W), F32),
             vmem((per, PR, W), F32),
             vmem((CORES * dps - 1, per, PR, W), F32),
-            vmem((3, W, W), BF16),
-            vmem((2, W, W), F32),
+            vmem((5, W, W), BF16),
+            vmem((8 * W, W), BF16),
+            vmem((W, W), BF16),
+            vmem((tiles, 8, W), F32),
             vmem((4, W, W), F32),
             vmem((W + 16, W), F32),
             vmem((3, W + 16, W), F32),
+            dma((6,)),
             dma((2,)),
-            dma((2,)),
-            dma(()),
+            dma((chips,)),
+            dma((chips,)),
             dma((chips,)),
             dma((2,)),
             dma((4,)),
@@ -382,27 +450,39 @@
             dma(()),
             dma(()),
             dma(()),
-            dma((3,)),
         ],
         compiler_params=pltpu.CompilerParams(
-            collective_id=0, has_side_effects=True, vmem_limit_bytes=48 * 1024 * 1024
+            collective_id=0, has_side_effects=True, vmem_limit_bytes=32 * 1024 * 1024
         ),
         cost_estimate=pl.CostEstimate(
             flops=6 * W * W * channels, bytes_accessed=16 * W * channels, transcendentals=0
         ),
         name="hyena_block",
     )(
-        x,
-        cotangent[0],
-        doc_ids,
-        short_taps.reshape(9, -1)[:, : W // 2],
-        long_taps[:4],
-        skip_gain.reshape(1, -1)[:, : W // 2],
+        *(
+            pltpu.with_memory_space_constraint(a, pltpu.HBM)
+            for a in (x, cotangent[0], doc_ids, short_taps, long_taps, skip_gain.reshape(1, -1))
+        )
     )
+    mixed, grad, short_grad, taps_grad, gain_grad = pl.pallas_call(
+        hand_over,
+        out_shape=(
+            jax.ShapeDtypeStruct((W, channels), BF16),
+            jax.ShapeDtypeStruct((3, W, channels), BF16),
+            jax.ShapeDtypeStruct((3, 3, W // 2), F32),
+            jax.ShapeDtypeStruct((4, W), F32),
+            jax.ShapeDtypeStruct((1, W // 2), F32),
+        ),
+        in_specs=[inv, inv],
+        out_specs=(any_, any_, inv, inv, inv),
+        scratch_shapes=[dma((4,))],
+        compiler_params=pltpu.CompilerParams(vmem_limit_bytes=16 * 1024 * 1024),
+        name="hand_over",
+    )(out, small)
     return (
         mixed[None],
         jnp.transpose(grad, (1, 0, 2))[None],
-        short_grad.reshape(3, 3, W // 2),
+        short_grad,
         taps_grad,
         gain_grad.reshape(W // 2),
     )

time: 79.1 us -> 60.4 us (0.76)
  local copies, waits for them, and re-layouts: 10.5 us -> 0 us
  Pallas kernels: 67.7 us -> 59.7 us
    pallas_call x1, Pallas kernels: 67.7 us -> 57.1 us  [local(): pl.pallas_call(functools.partial(kernel, tiles, chips, dps, scale), out_s...]
    unnamed x14 -> x0, local copies, waits for them, and re-layouts: 9.22 us -> none
    pallas_call x0 -> x1, Pallas kernels: none -> 2.64 us  [local(): pl.pallas_call(hand_over, out_shape=(jax.ShapeDtypeStruct((W, channels),...]
    reshape x2 -> x0, local copies, waits for them, and re-layouts: 1.3 us -> none  [the longest x1 0.7 us: local(): short_taps.reshape(9, -1)[:, :W // 2]]
where the time goes in v2:
time: 60.4 us; the launch traced here: 60.3 us
  Pallas kernels  59.7 us (99%)
  between operations  0.64 us (1%)
    pallas_call x1, Pallas kernels, local(): pl.pallas_call(functools.partial(kernel, tiles, chips, dps, scale), out_s...  57.1 us
    pallas_call x1, Pallas kernels, local(): pl.pallas_call(hand_over, out_shape=(jax.ShapeDtypeStruct((W, channels),...  2.64 us

profile of v2, /device:TPU:1, one launch (start us, length us, event | category | flops | bytes accessed | tf_op | source)
XLA Modules:
  0.0 60.3 jit_solution(7993117743217791883)
XLA Ops:
  0.6 57.1 %hyena_block.1 = (bf16[4,128,4096]{2,1,0:T(8,128)(2,1)S(1)}, f32[24,128]{1,0:T(8,128)S(1)}) custom-call(bf16[3,128,4096]{2,1,0:T(8,128)(2,1)} %bitcast.10, bf16[128,4096]{1,0:T(8,128)(2,1)} %bitcast.11, s32[1,128]{1,0:T(1,128)} %ids_hbm.1, f32[3,3,64]{2,1,0:T(4,128)} %short_hbm.1, f32[4,128]{1,0:T(4,128)} %taps_hbm.1, f32[1,64]{1,0:T(1,128)} %bitcast.12), custom_call_target="tpu_custom_call" | custom-call | flops 402653184 | bytes 8388608 | tf_op jit(solution)/shard_map/hyena_block/pallas_call | solution.py:395
  57.7 2.6 %hand_over.1 = (bf16[128,4096]{1,0:T(8,128)(2,1)}, bf16[3,128,4096]{2,1,0:T(8,128)(2,1)}, f32[3,3,64]{2,1,0:T(4,128)}, f32[4,128]{1,0:T(4,128)}, f32[1,64]{1,0:T(1,128)}) custom-call(bf16[4,128,4096]{2,1,0:T(8,128)(2,1)S(1)} %get-tuple-element.12.out, f32[24,128]{1,0:T(8,128)S(1)} %get-tuple-element.13.small), custom_call_target="tpu_custom_call" | custom-call | tf_op jit(solution)/shard_map/hand_over/pallas_call | solution.py:467

commit v3 on v2

--- a/solution.py
+++ b/solution.py
@@ -13,6 +13,7 @@
 W = 128
 PR = 18
 CORES = 2
+STEP = 32
 
 
 def dot(a, b, dims):
@@ -26,7 +27,7 @@
     x, cot, ids_ref, short_ref, taps_ref, gain_ref, act, g_own, c_own, g_prev, c_next,
     half, half_in, params, tail, tail_in, idp, idn, edge, edge_in, last,
     part, part_in, block, block_in,
-    bmask, perm, turn, rtaps, tmask, idx, shift,
+    bmask, perm, turn, rtaps, tmask, idx, shift, sums_t, turned, flat,
     load_sem, half_sem, par_send, par_pass, par_recv, tail_sem, id_sem,
     g_send, g_recv, c_send, c_recv, e_send, e_recv, r_send, r_recv, b_send, b_recv,
 ):
@@ -184,10 +185,9 @@
     load_c.wait()
     tail_to_next.wait()
 
-    def forward(i, carry):
+    def get_params(i):
         tile = lax.rem((chip + chips - 1) * per + i, tiles)
         owner = tile // per
-        lanes = pl.ds(pl.multiple_of(tile * W, W), W)
 
         far = lax.rem(chip + chips - owner, chips)
 
@@ -195,109 +195,155 @@
         def _():
             wait_bytes(params.at[pl.ds(0, per)], par_recv.at[owner])
 
+        return tile
+
+    def activate(tile, buf):
+        lanes = pl.ds(pl.multiple_of(tile * W, W), W)
         w = params[tile, 0:10]
         rtaps[tile] = dot(params[tile, 10:18].astype(BF16), turn[...], ((1,), (0,)))
-        m1, m2 = tmask[0], tmask[1]
+        g16, c16 = [], []
         for s in range(3):
-            now = x[s, :, lanes].astype(F32)
-            shift[s, 8 : W + 8] = now
-            shift[s, 6:8] = tail_in[2 * s : 2 * s + 2, lanes]
-            act[s, :, lanes] = (
-                w[3 * s : 3 * s + 1] * now
-                + w[3 * s + 1 : 3 * s + 2] * (shift[s, 7 : W + 7] * m1)
-                + w[3 * s + 2 : 3 * s + 3] * (shift[s, 6 : W + 6] * m2)
-            )
-        gated = act[1, :, lanes] * act[2, :, lanes]
-        cgrad = cot[:, lanes].astype(F32) * act[0, :, lanes]
-        g_own[tile] = gated.astype(BF16).T
-        c_own[tile] = cgrad.astype(BF16).T
+            shift[buf, s, 6:8] = tail_in[2 * s : 2 * s + 2, lanes]
+        for r in range(0, W, STEP):
+            rows = slice(r, r + STEP)
+            m1, m2 = tmask[0, rows], tmask[1, rows]
+            acts = []
+            for s in range(3):
+                now = x[s, rows, lanes].astype(F32)
+                shift[buf, s, 8 + r : 8 + r + STEP] = now
+                acts.append(
+                    w[3 * s : 3 * s + 1] * now
+                    + w[3 * s + 1 : 3 * s + 2] * (shift[buf, s, 7 + r : 7 + r + STEP] * m1)
+                    + w[3 * s + 2 : 3 * s + 3] * (shift[buf, s, 6 + r : 6 + r + STEP] * m2)
+                )
+                act[s, rows, lanes] = acts[s]
+            g16.append((acts[1] * acts[2]).astype(BF16))
+            c16.append((cot[rows, lanes].astype(F32) * acts[0]).astype(BF16))
+        g_own[tile] = jnp.concatenate(g16, axis=0).T
+        c_own[tile] = jnp.concatenate(c16, axis=0).T
+
+    def send_halo(tile):
         remote(g_own.at[tile], g_prev.at[tile], g_send, g_recv.at[tile], nxt).start()
         remote(c_own.at[tile], c_next.at[tile], c_send, c_recv.at[tile], prv).start()
+
+    def forward(i, carry):
+        pair = [get_params(2 * i + q) for q in range(2)]
+        for q in range(2):
+            activate(pair[q], q)
+        for q in range(2):
+            send_halo(pair[q])
         return carry
 
-    lax.fori_loop(0, tiles, forward, 0)
-
-    shift[:, W + 8 : W + 16] = jnp.zeros((3, 8, W), F32)
+    lax.fori_loop(0, tiles // 2, forward, 0)
+
+    shift[:, :, W + 8 : W + 16] = jnp.zeros((2, 3, 8, W), F32)
     lane_group = lax.broadcasted_iota(jnp.int32, (W, W), 1) // 16
 
     def circulant(row):
         spread = jnp.broadcast_to(row, (W, W))
         return pltpu.roll(spread, 0, 1, stride=1, stride_axis=0).astype(BF16)
 
-    def backward(i, carry):
-        tile = lax.rem(chip * per + i, tiles)
-        owner = tile // per
-        lanes = pl.ds(pl.multiple_of(tile * W, W), W)
+    def lanes_of(tile):
+        return pl.ds(pl.multiple_of(tile * W, W), W)
+
+    def tile_at(i):
+        return lax.rem(chip * per + i, tiles)
+
+    def arrived(tile):
         wait_bytes(g_prev.at[tile], g_recv.at[tile])
         wait_bytes(c_next.at[tile], c_recv.at[tile])
-        w = params[tile, 0:10]
+
+    def convolve(tile, buf):
+        lanes = lanes_of(tile)
         taps = params[tile, 10:18]
         flipped = rtaps[tile]
         k_own, k_prev, k_next, o_own, o_next = [bmask[q] for q in range(5)]
-        gated = act[1, :, lanes] * act[2, :, lanes]
-        g16 = gated.astype(BF16)
+        g16 = (act[1, :, lanes] * act[2, :, lanes]).astype(BF16)
         cc = jnp.concatenate([c_own[tile], c_next[tile]], axis=1)
         gg = jnp.concatenate([g_prev[tile], g_own[tile]], axis=1)
-        conv, back, pairs = [], [], []
         for g in range(8):
             fwd = circulant(taps[g : g + 1])
             rev = circulant(flipped[g : g + 1])
             rows = slice(16 * g, 16 * g + 16)
-            conv.append(
-                dot(gg[rows], jnp.concatenate([fwd * k_prev, fwd * k_own], axis=0), ((1,), (0,)))
+            weights = jnp.concatenate(
+                [
+                    jnp.concatenate([fwd * k_prev, fwd * k_own], axis=0),
+                    jnp.concatenate([rev * o_own, rev * o_next], axis=0),
+                ],
+                axis=1,
             )
-            back.append(
-                dot(cc[rows], jnp.concatenate([rev * o_own, rev * o_next], axis=0), ((1,), (0,)))
+            both_ways = dot(
+                jnp.concatenate([gg[rows], cc[rows]], axis=0), weights, ((1,), (0,))
             )
+            sums_t[buf, 0, rows] = both_ways[0:16, :W]
+            sums_t[buf, 1, rows] = both_ways[16:32, W:]
             pair = dot(jnp.where(lane_group == g, g16, jnp.zeros_like(g16)), cc, ((1,), (0,)))
             pair = pair.astype(BF16)
-            pairs.append(pair[:, :W] * k_own + pair[:, W:] * k_next)
-        lined = jnp.concatenate(
-            [
-                jnp.concatenate([pair[16 * q : 16 * q + 16] for pair in pairs], axis=0)
-                for q in range(8)
-            ],
-            axis=1,
-        )
-        diag = dot(lined, perm[...], ((1,), (0,)))
-        diag = [
-            jnp.sum(
-                pltpu.roll(diag[16 * g : 16 * g + 16], 0, 1, stride=1, stride_axis=0),
-                axis=0, keepdims=True,
-            )
-            for g in range(8)
-        ]
-        part[tile, 10:18] = jnp.concatenate(diag, axis=0)
-
+            pair = pair[:, :W] * k_own + pair[:, W:] * k_next
+            for q in range(8):
+                turned[buf, rows, q * W : q * W + W] = pair[16 * q : 16 * q + 16]
+
+    def combine(tile, buf):
+        flat[buf, 0] = sums_t[buf, 0].T
+        flat[buf, 1] = sums_t[buf, 1].T
+        lanes = lanes_of(tile)
+        w = params[tile, 0:10]
         gain = w[9:10]
-        q_act, k_act, v_act = act[0, :, lanes], act[1, :, lanes], act[2, :, lanes]
-        cotan = cot[:, lanes].astype(F32)
-        cgrad = cotan * q_act
-        convolved = jnp.concatenate(conv, axis=0).T + gain * gated
-        out[0, :, lanes] = (q_act * convolved).astype(BF16)
-        ggrad = jnp.concatenate(back, axis=0).T + gain * cgrad
-        u1, u2 = tmask[2], tmask[3]
-        sums = []
-        for s, ag in enumerate((cotan * convolved, ggrad * v_act, ggrad * k_act)):
-            shift[s, 8 : W + 8] = ag
-            edge[tile, 2 * s : 2 * s + 2] = ag[0:2]
-            b1 = shift[s, 9 : W + 9] * u1
-            b2 = shift[s, 10 : W + 10] * u2
-            sgrad = w[3 * s : 3 * s + 1] * ag + w[3 * s + 1 : 3 * s + 2] * b1 + w[3 * s + 2 : 3 * s + 3] * b2
-            out[s + 1, :, lanes] = sgrad.astype(BF16)
-            last[s, :, lanes] = sgrad[W - 16 :]
-            now = x[s, :, lanes].astype(F32)
-            before = tail_in[2 * s : 2 * s + 2, lanes]
-            a1 = ag[0:2] * tmask[0, 0:2]
-            a2 = ag[0:2] * tmask[1, 0:2]
-            sums.append(jnp.sum(now * ag, axis=0, keepdims=True))
-            sums.append(jnp.sum(now * b1, axis=0, keepdims=True) + a1[0:1] * before[1:2])
-            sums.append(
-                jnp.sum(now * b2, axis=0, keepdims=True) + a2[0:1] * before[0:1] + a2[1:2] * before[1:2]
-            )
-        sums.append(jnp.sum(cgrad * gated, axis=0, keepdims=True))
-        part[tile, 0:10] = jnp.concatenate(sums, axis=0)
+        sums = [jnp.zeros((8, W), F32)] * 10
+
+        def fold(a):
+            return jnp.sum(a.reshape(STEP // 8, 8, W), axis=0)
+
+        for r in range(W - STEP, -1, -STEP):
+            rows = slice(r, r + STEP)
+            q_act, k_act, v_act = act[0, rows, lanes], act[1, rows, lanes], act[2, rows, lanes]
+            gated = k_act * v_act
+            cotan = cot[rows, lanes].astype(F32)
+            cgrad = cotan * q_act
+            convolved = flat[buf, 0, rows] + gain * gated
+            ggrad = flat[buf, 1, rows] + gain * cgrad
+            out[0, rows, lanes] = (q_act * convolved).astype(BF16)
+            sums[9] = sums[9] + fold(cgrad * gated)
+            u1, u2 = tmask[2, rows], tmask[3, rows]
+            for s, ag in enumerate((cotan * convolved, ggrad * v_act, ggrad * k_act)):
+                shift[buf, s, 8 + r : 8 + r + STEP] = ag
+                b1 = shift[buf, s, 9 + r : 9 + r + STEP] * u1
+                b2 = shift[buf, s, 10 + r : 10 + r + STEP] * u2
+                sgrad = (
+                    w[3 * s : 3 * s + 1] * ag
+                    + w[3 * s + 1 : 3 * s + 2] * b1
+                    + w[3 * s + 2 : 3 * s + 3] * b2
+                )
+                out[s + 1, rows, lanes] = sgrad.astype(BF16)
+                now = x[s, rows, lanes].astype(F32)
+                for k, b in enumerate((ag, b1, b2)):
+                    sums[3 * s + k] = sums[3 * s + k] + fold(now * b)
+                if r == W - STEP:
+                    last[s, :, lanes] = sgrad[STEP - 16 :]
+                if r == 0:
+                    edge[tile, 2 * s : 2 * s + 2] = ag[0:2]
+        for q in range(10):
+            total = jnp.sum(sums[q], axis=0, keepdims=True)
+            if q < 9 and q % 3 > 0:
+                s = q // 3
+                head = shift[buf, s, 8:10] * tmask[q % 3 - 1, 0:2]
+                before = tail_in[2 * s : 2 * s + 2, lanes]
+                if q % 3 == 1:
+                    total = total + head[0:1] * before[1:2]
+                else:
+                    total = total + head[0:1] * before[0:1] + head[1:2] * before[1:2]
+            part[tile, q : q + 1] = total
         edge[tile, 6:8] = jnp.zeros((2, W), F32)
+
+    def skew(two):
+        diag = dot(turned[...].reshape(2 * W, 8 * W), perm[...], ((1,), (0,)))
+        for g in range(16):
+            row = pltpu.roll(diag[16 * g : 16 * g + 16], 0, 1, stride=1, stride_axis=0)
+            at = 10 + g % 8
+            part[two[g // 8], at : at + 1] = jnp.sum(row, axis=0, keepdims=True)
+
+    def send(tile):
+        owner = tile // per
         remote(edge.at[tile], edge_in.at[tile], e_send, e_recv, prv).start()
 
         @pl.when(owner != chip)
@@ -305,9 +351,30 @@
             slot = part_in.at[lax.rem(tile, per), lax.rem(chip + chips - owner, chips) - 1]
             remote(part.at[tile], slot, r_send, r_recv, owner * CORES + core).start()
 
+    def both(i, carry):
+        done = [tile_at(2 * i - 2 + q) for q in range(2)]
+        now = [tile_at(2 * i + q) for q in range(2)]
+        for q in range(2):
+            arrived(now[q])
+        skew(done)
+        for q in range(2):
+            combine(done[q], q)
+        for q in range(2):
+            convolve(now[q], q)
+        for q in range(2):
+            send(done[q])
         return carry
 
-    lax.fori_loop(0, tiles, backward, 0)
+    for q in range(2):
+        arrived(tile_at(q))
+    for q in range(2):
+        convolve(tile_at(q), q)
+    lax.fori_loop(1, tiles // 2, both, 0)
+    skew([tile_at(tiles - 2 + q) for q in range(2)])
+    for q in range(2):
+        combine(tile_at(tiles - 2 + q), q)
+    for q in range(2):
+        send(tile_at(tiles - 2 + q))
 
     wait_bytes(part_in, r_recv)
     for p in range(per):
@@ -340,7 +407,7 @@
             out[s + 1, W - 16 : W, lanes] = (last[s, :, lanes] + more).astype(BF16)
         return carry
 
-    lax.fori_loop(0, tiles, finish, 0)
+    lax.fori_loop(0, tiles, finish, 0, unroll=2)
     wait_bytes(block_in, b_recv)
     total = block[0]
     for d in range(CORES * dps - 1):
@@ -432,7 +499,10 @@
             vmem((tiles, 8, W), F32),
             vmem((4, W, W), F32),
             vmem((W + 16, W), F32),
-            vmem((3, W + 16, W), F32),
+            vmem((2, 3, W + 16, W), F32),
+            vmem((2, 2, W, W), F32),
+            vmem((2, W, 8 * W), BF16),
+            vmem((2, 2, W, W), F32),
             dma((6,)),
             dma((2,)),
             dma((chips,)),

time: 60.4 us -> 56.8 us (0.940)
  Pallas kernels: 59.7 us -> 56.1 us
    pallas_call x1, Pallas kernels: 57.1 us -> 53.4 us  [local(): pl.pallas_call(functools.partial(kernel, tiles, chips, dps, scale), out_s...]
where the time goes in v3:
time: 56.8 us; the launch traced here: 56.7 us
  Pallas kernels  56.1 us (99%)
  between operations  0.64 us (1%)
    pallas_call x1, Pallas kernels, local(): pl.pallas_call(functools.partial(kernel, tiles, chips, dps, scale), out_s...  53.4 us
    pallas_call x1, Pallas kernels, local(): pl.pallas_call(hand_over, out_shape=(jax.ShapeDtypeStruct((W, channels),...  2.64 us

profile of v3, /device:TPU:1, one launch (start us, length us, event | category | flops | bytes accessed | tf_op | source)
XLA Modules:
  0.0 56.7 jit_solution(16088841024540212427)
XLA Ops:
  0.6 53.4 %hyena_block.1 = (bf16[4,128,4096]{2,1,0:T(8,128)(2,1)S(1)}, f32[24,128]{1,0:T(8,128)S(1)}) custom-call(bf16[3,128,4096]{2,1,0:T(8,128)(2,1)} %bitcast.10, bf16[128,4096]{1,0:T(8,128)(2,1)} %bitcast.11, s32[1,128]{1,0:T(1,128)} %ids_hbm.1, f32[3,3,64]{2,1,0:T(4,128)} %short_hbm.1, f32[4,128]{1,0:T(4,128)} %taps_hbm.1, f32[1,64]{1,0:T(1,128)} %bitcast.12), custom_call_target="tpu_custom_call" | custom-call | flops 402653184 | bytes 8388608 | tf_op jit(solution)/shard_map/hyena_block/pallas_call | solution.py:462
  54.1 2.6 %hand_over.1 = (bf16[128,4096]{1,0:T(8,128)(2,1)}, bf16[3,128,4096]{2,1,0:T(8,128)(2,1)}, f32[3,3,64]{2,1,0:T(4,128)}, f32[4,128]{1,0:T(4,128)}, f32[1,64]{1,0:T(1,128)}) custom-call(bf16[4,128,4096]{2,1,0:T(8,128)(2,1)S(1)} %get-tuple-element.12.out, f32[24,128]{1,0:T(8,128)S(1)} %get-tuple-element.13.small), custom_call_target="tpu_custom_call" | custom-call | tf_op jit(solution)/shard_map/hand_over/pallas_call | solution.py:537

commit v4 on v3

--- a/solution.py
+++ b/solution.py
@@ -134,11 +134,11 @@
 
     def send_params(d):
         mine = params.at[pl.ds(chip * per, per)]
-        to = lax.rem(chip + d, chips) * CORES + core
+        to = lax.rem(chip + chips - d, chips) * CORES + core
         remote(mine, mine, par_send.at[d], par_recv.at[chip], to).start()
 
     def pass_params(d):
-        source = lax.rem(chip + chips - d, chips)
+        source = lax.rem(chip + d, chips)
         mine = params.at[pl.ds(source * per, per)]
         wait_bytes(mine, par_recv.at[source])
 
@@ -186,10 +186,10 @@
     tail_to_next.wait()
 
     def get_params(i):
-        tile = lax.rem((chip + chips - 1) * per + i, tiles)
+        tile = lax.rem(chip * per + i, tiles)
         owner = tile // per
 
-        far = lax.rem(chip + chips - owner, chips)
+        far = lax.rem(owner + chips - chip, chips)
 
         @pl.when((lax.rem(tile, per) == 0) & (lax.rem(far, peers) != place) & (far != 0))
         def _():
@@ -247,7 +247,7 @@
         return pl.ds(pl.multiple_of(tile * W, W), W)
 
     def tile_at(i):
-        return lax.rem(chip * per + i, tiles)
+        return lax.rem((chip + 1) * per + i, tiles)
 
     def arrived(tile):
         wait_bytes(g_prev.at[tile], g_recv.at[tile])

time: 56.8 us -> 55.2 us (0.972)
  Pallas kernels: 56.1 us -> 54.5 us
    pallas_call x1, Pallas kernels: 53.4 us -> 51.9 us  [local(): pl.pallas_call(functools.partial(kernel, tiles, chips, dps, scale), out_s...]
where the time goes in v4:
time: 55.2 us; the launch traced here: 55.1 us
  Pallas kernels  54.5 us (99%)
  between operations  0.64 us (1%)
    pallas_call x1, Pallas kernels, local(): pl.pallas_call(functools.partial(kernel, tiles, chips, dps, scale), out_s...  51.9 us
    pallas_call x1, Pallas kernels, local(): pl.pallas_call(hand_over, out_shape=(jax.ShapeDtypeStruct((W, channels),...  2.64 us

profile of v4, /device:TPU:1, one launch (start us, length us, event | category | flops | bytes accessed | tf_op | source)
XLA Modules:
  0.0 55.1 jit_solution(5473741005603525452)
XLA Ops:
  0.6 51.9 %hyena_block.1 = (bf16[4,128,4096]{2,1,0:T(8,128)(2,1)S(1)}, f32[24,128]{1,0:T(8,128)S(1)}) custom-call(bf16[3,128,4096]{2,1,0:T(8,128)(2,1)} %bitcast.10, bf16[128,4096]{1,0:T(8,128)(2,1)} %bitcast.11, s32[1,128]{1,0:T(1,128)} %ids_hbm.1, f32[3,3,64]{2,1,0:T(4,128)} %short_hbm.1, f32[4,128]{1,0:T(4,128)} %taps_hbm.1, f32[1,64]{1,0:T(1,128)} %bitcast.12), custom_call_target="tpu_custom_call" | custom-call | flops 402653184 | bytes 8388608 | tf_op jit(solution)/shard_map/hyena_block/pallas_call | solution.py:462
  52.5 2.6 %hand_over.1 = (bf16[128,4096]{1,0:T(8,128)(2,1)}, bf16[3,128,4096]{2,1,0:T(8,128)(2,1)}, f32[3,3,64]{2,1,0:T(4,128)}, f32[4,128]{1,0:T(4,128)}, f32[1,64]{1,0:T(1,128)}) custom-call(bf16[4,128,4096]{2,1,0:T(8,128)(2,1)S(1)} %get-tuple-element.12.out, f32[24,128]{1,0:T(8,128)S(1)} %get-tuple-element.13.small), custom_call_target="tpu_custom_call" | custom-call | tf_op jit(solution)/shard_map/hand_over/pallas_call | solution.py:537
